TPU v7x, 32 devices: a whole 2x2x4 slice. The times are simulated.
32 devices in a mesh: dp: 4 (over z), mp: 8 (over y, x, core).
Axes of the slice: x: 2, y: 2, z: 4, core: 2. Of those that a mesh axis runs over, the one named last changes fastest.
Arguments:
- gradient: bfloat16 [4, 8192, 8192], P('dp', 'mp'), may hold values from -6 to 6
- error: bfloat16 [4, 8192, 8192], P('dp', 'mp'), may hold values from -4 to 4
- query: bfloat16 [8192, 256], P('mp'), may hold values from -0.0625 to 0.0625
Outputs:
- factor: float32 [8192, 256], P('mp')
- new_error: bfloat16 [4, 8192, 8192], P('dp', 'mp')
All inputs are finite; a program needn't handle non-finite values.
Results may differ from a plain program's by a relative error of at most 0.013.
Values may be sent and summed in bfloat16 or wider, within the bound.
A program may use at most 128 MiB of HBM per device.

v0:
```python
import jax
import jax.numpy as jnp
from jax import lax
from jax.sharding import PartitionSpec as P


def orthonormal(rows_proj, gram):
    lower = jnp.linalg.cholesky(gram)
    return lax.linalg.triangular_solve(
        lower, rows_proj, left_side=False, lower=True, transpose_a=True
    ).astype(jnp.bfloat16)


def gram_of(rows_proj):
    return jnp.dot(rows_proj.T, rows_proj, precision=lax.Precision.HIGHEST)


def shards(gradient, error, query):
    adjusted = (gradient[0].astype(jnp.float32) + error[0].astype(jnp.float32)).astype(jnp.bfloat16)
    cols_dev = query.shape[0]
    replicas = lax.axis_size("dp")
    projection = jnp.dot(
        adjusted,
        lax.all_gather(query, "mp", axis=0, tiled=True),
        preferred_element_type=jnp.float32,
    )
    summed = lax.psum(projection, "dp")
    gram = lax.psum(gram_of(summed).astype(jnp.bfloat16), "mp").astype(jnp.float32)
    basis = orthonormal(summed, gram)
    contract = (((0,), (0,)), ((), ()))
    term = lax.dot_general(adjusted, basis, contract, preferred_element_type=jnp.float32)
    factor_full = lax.psum(term, ("dp", "mp")) / replicas
    factor_half = factor_full.astype(jnp.bfloat16)
    own = lax.dynamic_slice_in_dim(factor_full, lax.axis_index("mp") * cols_dev, cols_dev, 0)
    approx = lax.dot_general(
        basis, factor_half, (((1,), (1,)), ((), ())), preferred_element_type=jnp.float32
    )
    new_error = (adjusted.astype(jnp.float32) - approx).astype(jnp.bfloat16)
    return (own, new_error[None])


def solution(mesh):
    in_specs = (P("dp", "mp", None), P("dp", "mp", None), P("mp", None))
    out_specs = (P("mp", None), P("dp", "mp", None))
    return jax.shard_map(shards, mesh=mesh, in_specs=in_specs, out_specs=out_specs, check_vma=False)
```

profile of v0, /device:TPU:0, one launch (start us, length us, event | category | flops | bytes accessed | tf_op | source)
XLA Modules:
  0.0 473.5 jit_solution(1836420825661314490)
XLA Ops:
  7.2 0.7 all-gather.2.cloned.1.call-update
  7.9 0.0 all-reduce.5.cloned.1.call-start
  7.9 41.4 %all-gather.2.cloned.1.call-done = bf16[8192,256]{1,0:T(8,128)(2,1)} async-done(((bf16[1024,256]{1,0:T(8,128)(2,1)}), bf16[8192,256]{1,0:T(8,128)(2,1)}) %all-gather.2.cloned.1.call-update) | async-done | bytes 4194320 | tf_op jit(solution)/shard_map/all_gather | solution.py:24
  49.3 17.2 %fusion.14 = f32[1024,256]{1,0:T(8,128)} fusion(bf16[8192,256]{1,0:T(8,128)(2,1)} %all-gather.2.cloned.1.call-done, bf16[1,1024,8192]{2,1,0:T(8,128)(2,1)} %param.4, bf16[1,1024,8192]{2,1,0:T(8,128)(2,1)} %param.3), kind=kOutput, calls=%fused_computation.39 | convolution fusion | flops 4328521728 | bytes 38797312 | tf_op jit(solution)/shard_map/dot_general | solution.py:22
  66.6 0.0 all-reduce.7.cloned.1.call-start
  66.6 51.9 %all-reduce.5.cloned.1.call-done = f32[1024,256]{1,0:T(8,128)} async-done(((f32[1024,256]{1,0:T(8,128)}), f32[1024,256]{1,0:T(8,128)}) %all-reduce.5.cloned.1.call-update) | async-done | bytes 1048592 | tf_op jit(solution)/shard_map/psum | solution.py:27
  118.6 4.0 convolution_convert_fusion.1
  122.6 0.2 all-reduce.9.cloned.1.call-start
  122.8 52.2 %all-reduce.7.cloned.1.call-done = bf16[256,256]{0,1:T(8,128)(2,1)} async-done(((bf16[256,256]{0,1:T(8,128)(2,1)}), bf16[256,256]{0,1:T(8,128)(2,1)}) %all-reduce.7.cloned.1.call-update) | async-done | bytes 131088 | tf_op jit(solution)/shard_map/psum | solution.py:28
  175.1 1.0 copy.6
  176.1 0.9 fusion.6
  177.0 11.7 %cholesky.50 = f32[128,128]{1,0:T(8,128)S(1)} custom-call(f32[128,128]{1,0:T(8,128)S(1)} %cholesky.118), custom_call_target="Cholesky" | custom-call | tf_op jit(solution)/shard_map/jit(cholesky)/cholesky | solution.py:8
  188.8 9.8 %custom-call.14 = f32[1,128,128]{1,2,0:T(8,128)S(1)} custom-call(f32[1,128,128]{2,1,0:T(8,128)S(1)} %get-tuple-element.23), custom_call_target="InvertDiagBlocksLowerTriangular" | custom-call | tf_op jit(solution)/shard_map/jit(cholesky)/cholesky | solution.py:8
  198.6 0.2 constant_dynamic-update-slice_fusion
  198.8 0.3 convolution_subtract_fusion.1
  199.1 11.7 %cholesky.105 = f32[128,128]{1,0:T(8,128)S(1)} custom-call(f32[128,128]{1,0:T(8,128)S(1)} %convolution_subtract_fusion.1), custom_call_target="Cholesky" | custom-call | tf_op jit(solution)/shard_map/jit(cholesky)/cholesky | solution.py:8
  210.9 0.7 compare_reduce_fusion
  213.0 0.1 triangular_solve.58
  213.0 4.1 while.1
  213.0 0.6 fusion.26
  213.6 1.4 bitcast_dynamic-update-slice_fusion.2
  215.1 0.6 fusion.26
  215.7 1.4 bitcast_dynamic-update-slice_fusion.2
  217.1 19.9 %custom-call.15 = f32[2,128,128]{1,2,0:T(8,128)S(1)} custom-call(f32[2,128,128]{2,1,0:T(8,128)S(1)} %get-tuple-element.9), custom_call_target="InvertDiagBlocksLowerTriangular" | custom-call | tf_op jit(solution)/shard_map/triangular_solve | solution.py:9
  237.0 1.7 fusion.17
  238.7 2.0 convolution_subtract_fusion
  240.8 0.6 convolution_convert_fusion
  241.4 21.8 %fusion.5 = f32[8192,256]{1,0:T(8,128)} fusion(bf16[1024,128]{0,1:T(8,128)(2,1)S(1)} %convolution_convert_fusion, bf16[1024,128]{0,1:T(8,128)(2,1)S(1)} %get-tuple-element.26, bf16[1,1024,8192]{2,1,0:T(8,128)(2,1)} %param.4, bf16[1,1024,8192]{2,1,0:T(8,128)(2,1)} %param.3), kind=kOutput, calls=%fused_computation.15 | convolution fusion | flops 4329570304 | bytes 42467328 | tf_op jit(solution)/shard_map/dot_general | solution.py:31
  263.2 178.1 %all-reduce.9.cloned.1.call-done = f32[8192,256]{1,0:T(8,128)} async-done(((f32[8192,256]{1,0:T(8,128)}), f32[8192,256]{1,0:T(8,128)}) %all-reduce.9.cloned.1.call-update) | async-done | bytes 8388624 | tf_op jit(solution)/shard_map/psum | solution.py:32
  441.3 3.9 broadcast_multiply_fusion
  445.2 1.0 constant_dynamic-slice_fusion.1
  446.2 20.8 %fusion.1 = bf16[1,1024,8192]{2,1,0:T(8,128)(2,1)} fusion(bf16[1024,128]{0,1:T(8,128)(2,1)S(1)} %convolution_convert_fusion, bf16[1024,128]{0,1:T(8,128)(2,1)S(1)} %get-tuple-element.26, f32[8192,256]{1,0:T(8,128)} %all-reduce.9.cloned.1.call-done, bf16[1,1024,8192]{2,1,0:T(8,128)(2,1)} %param.4, bf16[1,1024,8192]{2,1,0:T(8,128)(2,1)} %param.3), kind=kOutput, calls=%fused_computation.5 | convolution fusion | flops 4358930432 | bytes 59244544 | tf_op jit(solution)/shard_map/dot_general | solution.py:35
  (13 shorter events, 0.2 us)
Async XLA Ops:
  7.2 42.2 %all-gather.2.cloned.1.call-start = ((), (), s32[]{:S(2)}) async-start(), calls=%async_computation | async-start | bytes 4718592 | tf_op jit(solution)/shard_map/all_gather | solution.py:24
  7.9 110.7 %all-reduce.5.cloned.1.call-start = ((), (), s32[]{:S(2)}) async-start(), calls=%async_computation.1 | async-start | bytes 2097152 | tf_op jit(solution)/shard_map/psum | solution.py:27
  66.6 108.5 %all-reduce.7.cloned.1.call-start = ((), (), s32[]{:S(2)}) async-start(), calls=%async_computation.2 | async-start | bytes 262144 | tf_op jit(solution)/shard_map/psum | solution.py:28
  122.6 318.7 %all-reduce.9.cloned.1.call-start = ((), (), s32[]{:S(2)}) async-start(), calls=%async_computation.3 | async-start | bytes 16777216 | tf_op jit(solution)/shard_map/psum | solution.py:32
Sparse Core Ops, SparseCore 0:
  9.9 39.4 all-gather.1
  66.7 51.8 all-reduce.4
  122.7 52.3 all-reduce.6
  263.3 177.9 all-reduce.8
where the time goes:
time: 474 us
  waiting for transfers between devices  324 us (68%)
  matrix products  68.6 us (14%)
  other arithmetic  58.8 us (12%)
  between operations  15.2 us (3%)
  local copies, waits for them, and re-layouts  6.2 us (1%)
    psum x1, waiting for transfers between devices, shards(): factor_full = lax.psum(term, ('dp', 'mp')) / replicas  178 us
    psum x1, waiting for transfers between devices, shards(): lax.psum(gram_of(summed).astype(jnp.bfloat16), 'mp').astype(jnp.float32)  52.2 us
    psum x1, waiting for transfers between devices, shards(): summed = lax.psum(projection, 'dp')  51.9 us
    all_gather x1, waiting for transfers between devices, shards(): lax.all_gather(query, 'mp', axis=0, tiled=True)  41.4 us
    another operation x6, other arithmetic, orthonormal(): lower = jnp.linalg.cholesky(gram)  34 us
    dot_general x1, matrix products, shards(): lax.dot_general(adjusted, basis, contract, preferred_element_type=jnp.flo...  21.8 us
    dot_general x1, matrix products, shards(): lax.dot_general(basis, factor_half, (((1,), (1,)), ((), ())), preferred_e...  20.8 us
    another operation x3, other arithmetic, orthonormal(): lax.linalg.triangular_solve(lower, rows_proj, left_side=False, lower=True...  19.9 us
  transfers between devices with their start and end apart: 4, of which 4 were waited for; matrix products, arithmetic and copies ran while one was open for 0% of the time, Pallas kernels for 0%

commit v1 on v0

v1 whole, which is shorter than its diff:
```python
import functools

import jax
import jax.numpy as jnp
from jax import lax
from jax.experimental import pallas as pl
from jax.experimental.pallas import tpu as pltpu
from jax.sharding import PartitionSpec as P

F32, BF16 = jnp.float32, jnp.bfloat16
PANEL, GROUP = 32, 4


def dot_hi(a, b, dims):
    return lax.dot_general(a, b, (dims, ((), ())), precision=lax.Precision.HIGHEST, preferred_element_type=F32)


def inverse_of_panel(block):
    size = block.shape[0]
    eye = (lax.broadcasted_iota(jnp.int32, (size, size), 0) == lax.broadcasted_iota(jnp.int32, (size, size), 1)).astype(F32)
    work = jnp.concatenate([block, eye, jnp.zeros((size, 128 - 2 * size), F32)], axis=1)
    row_id = lax.broadcasted_iota(jnp.int32, (size, 128), 0)
    scale = jnp.zeros((size, 128), F32)
    for start in range(0, size, GROUP):
        ids = range(start, start + GROUP)
        cols = [jnp.broadcast_to(work[:, k:k + 1], (size, 128)) for k in ids]
        rows = [work[k:k + 1, :] for k in ids]
        pivots = [[jnp.broadcast_to(work[k:k + 1, l:l + 1], (1, 128)) for l in ids] for k in ids]
        for j, k in enumerate(ids):
            recip = 1.0 / pivots[j][j]
            scale = jnp.where(row_id == k, pivots[j][j], scale)
            work = work - jnp.where(row_id > k, cols[j] * recip, 0.0) * rows[j]
            for i in range(j + 1, GROUP):
                ratio = pivots[j][i] * recip
                cols[i] = cols[i] - cols[j] * ratio
                rows[i] = rows[i] - rows[j] * ratio
                for l in range(i, GROUP):
                    pivots[i][l] = pivots[i][l] - ratio * pivots[j][l]
    return (work * lax.rsqrt(scale))[:, size:2 * size]


def inverse_kernel(gram_ref, out_ref, work):
    rank = gram_ref.shape[0]
    work[:, :rank] = gram_ref[...]
    work[:, rank:] = (lax.broadcasted_iota(jnp.int32, (rank, rank), 0) == lax.broadcasted_iota(jnp.int32, (rank, rank), 1)).astype(F32)
    for start in range(0, rank, PANEL):
        stop = start + PANEL
        inverse = inverse_of_panel(work[start:stop, start:stop])
        panel = dot_hi(inverse, work[start:stop, :], ((1,), (0,)))
        out_ref[start:stop, :] = panel[:, rank:]
        if stop < rank:
            work[stop:, :] = work[stop:, :] - dot_hi(panel[:, stop:rank], panel, ((0,), (0,)))


def inverse_factor(gram):
    rank = gram.shape[0]
    return pl.pallas_call(
        inverse_kernel,
        out_shape=jax.ShapeDtypeStruct((rank, rank), F32),
        in_specs=[pl.BlockSpec(memory_space=pltpu.VMEM)],
        out_specs=pl.BlockSpec(memory_space=pltpu.VMEM),
        scratch_shapes=[pltpu.VMEM((rank, 2 * rank), F32)],
        compiler_params=pltpu.CompilerParams(vmem_limit_bytes=16 * 2**20),
    )(gram)


def swap(value, step):
    axis, bit = step
    return lax.ppermute(value, axis, [(i, i ^ bit) for i in range(lax.axis_size(axis))])


def upper(step):
    return (lax.axis_index(step[0]) // step[1]) % 2


def bits(axis):
    return [(axis, 1 << b) for b in range(lax.axis_size(axis).bit_length() - 1)]


def scatter_sum(value, steps):
    for step in steps:
        half, mine = value.shape[0] // 2, upper(step)
        sent = lax.dynamic_slice_in_dim(value, (1 - mine) * half, half, 0).astype(BF16)
        got = swap(sent, step)
        value = lax.dynamic_slice_in_dim(value, mine * half, half, 0).astype(F32) + got.astype(F32)
    return value


def joined(value, step, axis):
    got, mine = swap(value, step), upper(step) == 1
    return jnp.concatenate([jnp.where(mine, got, value), jnp.where(mine, value, got)], axis=axis)


def gather(value, steps):
    for step in reversed(steps):
        value = joined(value, step, 0)
    return value


def gather_blocks(value, order, steps):
    value = value.reshape((1,) * len(steps) + value.shape)
    for place in order:
        value = joined(value, steps[place], len(steps) - 1 - place)
    return value.reshape((-1,) + value.shape[len(steps):])


def shards(gradient, error, query):
    replicas = lax.axis_size("dp")
    mp, dp = bits("mp"), bits("dp")
    adjusted = (gradient[0].astype(F32) + error[0].astype(F32)).astype(BF16)
    half = query.shape[0] // 2
    forth = list(range(1, len(mp))) + [0]
    back = list(range(len(mp) - 1, 0, -1)) + [0]
    whole = jnp.concatenate(
        [gather_blocks(query[:half], forth, mp), gather_blocks(query[half:], back, mp)], axis=1
    ).reshape(-1, query.shape[1])
    projection = jnp.dot(adjusted, whole, preferred_element_type=F32)
    summed = gather(scatter_sum(projection, dp).astype(BF16), dp)
    gram = lax.dot_general(summed, summed, (((0,), (0,)), ((), ())), preferred_element_type=F32)
    for step in mp:
        gram = gram + swap(gram, step)
    inverse = inverse_factor(gram)
    basis = dot_hi(summed.astype(F32), inverse, ((1,), (1,))).astype(BF16)
    term = lax.dot_general(adjusted, basis, (((0,), (0,)), ((), ())), preferred_element_type=F32)
    first = scatter_sum(term, mp[:1])
    cut = first.shape[0] // 2
    one, two = mp[1:] + dp, mp[:0:-1] + dp
    parts = [(first[:cut], one), (first[cut:], two)]
    gathered = [
        gather((scatter_sum(part, steps) / replicas).astype(BF16), steps) for part, steps in parts
    ]
    factor_half = gather(jnp.concatenate(gathered, axis=0), mp[:1])
    own = lax.dynamic_slice_in_dim(
        factor_half, lax.axis_index("mp") * query.shape[0], query.shape[0], 0
    ).astype(F32)
    approx = lax.dot_general(basis, factor_half, (((1,), (1,)), ((), ())), preferred_element_type=F32)
    new_error = (adjusted.astype(F32) - approx).astype(BF16)
    return (own, new_error[None])


def solution(mesh):
    in_specs = (P("dp", "mp", None), P("dp", "mp", None), P("mp", None))
    out_specs = (P("mp", None), P("dp", "mp", None))
    return jax.shard_map(shards, mesh=mesh, in_specs=in_specs, out_specs=out_specs, check_vma=False)
```

time: 474 us -> 254 us (0.54)
  waiting for transfers between devices: 324 us -> 122 us
  other arithmetic: 58.8 us -> 24.9 us
  starting transfers between devices: 0.34 us -> 27.6 us
  between operations: 15.2 us -> 1.05 us
  Pallas kernels: 0 us -> 13.3 us
  matrix products: 68.6 us -> 58.4 us
    psum x3 -> x0, waiting for transfers between devices: 282 us -> none  [the longest x1 178 us: shards(): factor_full = lax.psum(term, ('dp', 'mp')) / replicas]
    ppermute x0 -> x31, waiting for transfers between devices: none -> 122 us  [swap(): lax.ppermute(value, axis, [(i, i ^ bit) for i in range(lax.axis_size(axis...]
    another operation x9 -> x0, other arithmetic: 54 us -> none  [the longest x6 34 us: orthonormal(): lower = jnp.linalg.cholesky(gram)]
    all_gather x1 -> x0, waiting for transfers between devices: 41.4 us -> none  [shards(): lax.all_gather(query, 'mp', axis=0, tiled=True)]
    ppermute x0 -> x31, starting transfers between devices: none -> 27.6 us  [swap(): lax.ppermute(value, axis, [(i, i ^ bit) for i in range(lax.axis_size(axis...]
    pallas_call x0 -> x1, Pallas kernels: none -> 13.3 us  [inverse_factor(): pl.pallas_call(inverse_kernel, out_shape=jax.ShapeDtypeStruct((rank, rank...]
    select_n x0 -> x15, other arithmetic: none -> 11.8 us  [joined(): jnp.where(mine, got, value)]
    add x0 -> x11, other arithmetic: none -> 6.19 us  [the longest x8 6.08 us: scatter_sum(): lax.dynamic_slice_in_dim(value, mine * half, half, 0).astype(F32)]
  transfers between devices with their start and end apart: 4 -> 31, of which waited for: 4 -> 30; matrix products, arithmetic and copies ran while one was open for 0% -> 2% of each run, Pallas kernels for 0% -> 0%
where the time goes in v1:
time: 254 us; the launch traced here: 253 us
  waiting for transfers between devices  122 us (48%)
  matrix products  58.4 us (23%)
  starting transfers between devices  27.6 us (11%)
  other arithmetic  24.9 us (10%)
  Pallas kernels  13.3 us (5%)
  local copies, waits for them, and re-layouts  6.18 us (2%)
    ppermute x31, waiting for transfers between devices, swap(): lax.ppermute(value, axis, [(i, i ^ bit) for i in range(lax.axis_size(axis...  122 us
    ppermute x31, starting transfers between devices, swap(): lax.ppermute(value, axis, [(i, i ^ bit) for i in range(lax.axis_size(axis...  27.6 us
    dot_general x1, matrix products, shards(): lax.dot_general(adjusted, basis, (((0,), (0,)), ((), ())), preferred_elem...  22.2 us
    dot_general x1, matrix products, shards(): lax.dot_general(basis, factor_half, (((1,), (1,)), ((), ())), preferred_e...  20.9 us
    dot_general x1, matrix products, shards(): projection = jnp.dot(adjusted, whole, preferred_element_type=F32)  14.3 us
    pallas_call x1, Pallas kernels, inverse_factor(): pl.pallas_call(inverse_kernel, out_shape=jax.ShapeDtypeStruct((rank, rank...  13.3 us
    select_n x15, other arithmetic, joined(): jnp.where(mine, got, value)  11.8 us
    add x8, other arithmetic, scatter_sum(): lax.dynamic_slice_in_dim(value, mine * half, half, 0).astype(F32)  6.08 us
  transfers between devices with their start and end apart: 31, of which 30 were waited for; matrix products, arithmetic and copies ran while one was open for 2% of the time, Pallas kernels for 0%

profile of v1, /device:TPU:0, one launch (start us, length us, event | category | flops | bytes accessed | tf_op | source)
XLA Modules:
  0.0 253.2 jit_solution(15490938958320077948)
XLA Ops:
  1.7 3.0 %collective-permute-start = (bf16[1,1,1,512,256]{4,3,2,1,0:T(8,128)(2,1)S(1)}, bf16[1,1,1,512,256]{4,3,2,1,0:T(8,128)(2,1)S(1)}, u32[]{:S(2)}, u32[]{:S(2)}) collective-permute-start(bf16[1,1,1,512,256]{4,3,2,1,0:T(8,128)(2,1)S(1)} %get-tuple-element.30), channel_id=1, source_target_pairs={{0,2},{1,3},{2,0},{3,1},{4,6},{5,7},{6,4},{7,5},{8,10},{9,11},{10,... | collective-permute-start | bytes 786440 | tf_op jit(solution)/shard_map/ppermute | solution.py:69
  6.2 4.8 %collective-permute-done = bf16[1,1,1,512,256]{4,3,2,1,0:T(8,128)(2,1)S(1)} collective-permute-done((bf16[1,1,1,512,256]{4,3,2,1,0:T(8,128)(2,1)S(1)}, bf16[1,1,1,512,256]{4,3,2,1,0:T(8,128)(2,1)S(1)}, u32[]{:S(2)}, u32[]{:S(2)}) %collective-permute-start) | collective-permute-done | bytes 262176 | tf_op jit(solution)/shard_map/ppermute | solution.py:69
  15.9 10.3 %collective-permute-done.1 = bf16[1,2,1,512,256]{4,3,2,1,0:T(8,128)(2,1)S(1)} collective-permute-done((bf16[1,2,1,512,256]{4,3,2,1,0:T(8,128)(2,1)S(1)}, bf16[1,2,1,512,256]{4,3,2,1,0:T(8,128)(2,1)S(1)}, u32[]{:S(2)}, u32[]{:S(2)}) %collective-permute-start.1) | collective-permute-done | bytes 524320 | tf_op jit(solution)/shard_map/ppermute | solution.py:69
  30.2 1.6 collective-permute-done.5
  33.7 2.3 pad_maximum_fusion.2
  36.0 14.3 %fusion.10 = f32[1024,256]{1,0:T(8,128)S(1)} fusion(bf16[8192,256]{1,0:T(8,128)(2,1)} %bitcast.29, bf16[1,1024,8192]{2,1,0:T(8,128)(2,1)} %param.4, bf16[1,1024,8192]{2,1,0:T(8,128)(2,1)} %param.3), kind=kOutput, calls=%fused_computation.89 | convolution fusion | flops 4328521728 | bytes 38797312 | tf_op jit(solution)/shard_map/dot_general | solution.py:117
  50.4 1.6 collective-permute-start.6
  52.0 6.8 %collective-permute-done.6 = bf16[512,256]{1,0:T(8,128)(2,1)S(1)} collective-permute-done((bf16[512,256]{1,0:T(8,128)(2,1)S(1)}, bf16[512,256]{1,0:T(8,128)(2,1)S(1)}, u32[]{:S(2)}, u32[]{:S(2)}) %collective-permute-start.6) | collective-permute-done | bytes 262176 | tf_op jit(solution)/shard_map/ppermute | solution.py:69
  58.9 2.7 %collective-permute-start.7 = (bf16[256,256]{1,0:T(8,128)(2,1)S(1)}, bf16[256,256]{1,0:T(8,128)(2,1)S(1)}, u32[]{:S(2)}, u32[]{:S(2)}) collective-permute-start(bf16[256,256]{1,0:T(8,128)(2,1)S(1)} %dynamic-slice_convert_fusion.8), channel_id=1, source_target_pairs={{0,16},{8,24},{16,0},{24,8},{1,17},{9,25},{17,1},{25,9},{2,18},{10... | collective-permute-start | bytes 393224 | tf_op jit(solution)/shard_map/ppermute | solution.py:69
  61.6 5.8 %collective-permute-done.7 = bf16[256,256]{1,0:T(8,128)(2,1)S(1)} collective-permute-done((bf16[256,256]{1,0:T(8,128)(2,1)S(1)}, bf16[256,256]{1,0:T(8,128)(2,1)S(1)}, u32[]{:S(2)}, u32[]{:S(2)}) %collective-permute-start.7) | collective-permute-done | bytes 131104 | tf_op jit(solution)/shard_map/ppermute | solution.py:69
  67.5 8.5 %collective-permute-done.8 = bf16[256,256]{1,0:T(8,128)(2,1)S(1)} collective-permute-done((bf16[256,256]{1,0:T(8,128)(2,1)S(1)}, bf16[256,256]{1,0:T(8,128)(2,1)S(1)}, u32[]{:S(2)}, u32[]{:S(2)}) %collective-permute-start.8) | collective-permute-done | bytes 131104 | tf_op jit(solution)/shard_map/ppermute | solution.py:69
  76.1 6.4 %collective-permute-done.9 = bf16[512,256]{1,0:T(8,128)(2,1)S(1)} collective-permute-done((bf16[512,256]{1,0:T(8,128)(2,1)S(1)}, bf16[512,256]{1,0:T(8,128)(2,1)S(1)}, u32[]{:S(2)}, u32[]{:S(2)}) %collective-permute-start.9) | collective-permute-done | bytes 262176 | tf_op jit(solution)/shard_map/ppermute | solution.py:69
  85.2 7.7 %collective-permute-done.11 = f32[256,256]{1,0:T(8,128)S(1)} collective-permute-done((f32[256,256]{1,0:T(8,128)S(1)}, f32[256,256]{1,0:T(8,128)S(1)}, u32[]{:S(2)}, u32[]{:S(2)}) %collective-permute-start.11) | collective-permute-done | bytes 262176 | tf_op jit(solution)/shard_map/ppermute | solution.py:69
  94.6 6.0 %collective-permute-done.12 = f32[256,256]{1,0:T(8,128)S(1)} collective-permute-done((f32[256,256]{1,0:T(8,128)S(1)}, f32[256,256]{1,0:T(8,128)S(1)}, u32[]{:S(2)}, u32[]{:S(2)}) %collective-permute-start.12) | collective-permute-done | bytes 262176 | tf_op jit(solution)/shard_map/ppermute | solution.py:69
  100.6 13.3 %shard_map.50 = f32[256,256]{1,0:T(8,128)S(1)} custom-call(f32[256,256]{1,0:T(8,128)S(1)} %add.166.gram_ref), custom_call_target="tpu_custom_call" | custom-call | tf_op jit(solution)/shard_map/pallas_call | solution.py:57
  114.6 22.2 %fusion.8 = f32[8192,256]{1,0:T(8,128)} fusion(bf16[1024,256]{1,0:T(8,128)(2,1)S(1)} %convolution_convert_fusion, bf16[1,1024,8192]{2,1,0:T(8,128)(2,1)} %param.4, bf16[1,1024,8192]{2,1,0:T(8,128)(2,1)} %param.3), kind=kOutput, calls=%fused_computation.88 | convolution fusion | flops 4328521728 | bytes 42467328 | tf_op jit(solution)/shard_map/dot_general | solution.py:124
  136.8 2.4 dynamic-slice_convert_fusion
  139.3 4.3 %collective-permute-done.13 = bf16[4096,256]{1,0:T(8,128)(2,1)} collective-permute-done((bf16[4096,256]{1,0:T(8,128)(2,1)S(1)}, bf16[4096,256]{1,0:T(8,128)(2,1)}, u32[]{:S(2)}, u32[]{:S(2)}) %collective-permute-start.13) | collective-permute-done | bytes 2097184 | tf_op jit(solution)/shard_map/ppermute | solution.py:69
  143.5 3.2 %convert_add_fusion = f32[4096,256]{1,0:T(8,128)S(1)} fusion(bf16[4096,256]{1,0:T(8,128)(2,1)} %collective-permute-done.13, f32[8192,256]{1,0:T(8,128)} %fusion.8, s32[]{:T(128)S(6)} %select_n.387), kind=kLoop, calls=%fused_computation.8 | loop fusion | flops 2097152 | bytes 10485764 | tf_op jit(solution)/shard_map/add | solution.py:85
  150.7 11.8 %collective-permute-done.14 = bf16[1024,256]{1,0:T(8,128)(2,1)} collective-permute-done((bf16[1024,256]{1,0:T(8,128)(2,1)S(1)}, bf16[1024,256]{1,0:T(8,128)(2,1)}, u32[]{:S(2)}, u32[]{:S(2)}) %collective-permute-start.14) | collective-permute-done | bytes 524320 | tf_op jit(solution)/shard_map/ppermute | solution.py:69
  167.5 4.1 %collective-permute-done.15 = bf16[512,256]{1,0:T(8,128)(2,1)S(1)} collective-permute-done((bf16[512,256]{1,0:T(8,128)(2,1)S(1)}, bf16[512,256]{1,0:T(8,128)(2,1)S(1)}, u32[]{:S(2)}, u32[]{:S(2)}) %collective-permute-start.15) | collective-permute-done | bytes 262176 | tf_op jit(solution)/shard_map/ppermute | solution.py:69
  172.1 2.1 collective-permute-done.23
  174.6 3.2 %collective-permute-done.16 = bf16[256,256]{1,0:T(8,128)(2,1)S(1)} collective-permute-done((bf16[256,256]{1,0:T(8,128)(2,1)S(1)}, bf16[256,256]{1,0:T(8,128)(2,1)S(1)}, u32[]{:S(2)}, u32[]{:S(2)}) %collective-permute-start.16) | collective-permute-done | bytes 131104 | tf_op jit(solution)/shard_map/ppermute | solution.py:69
  181.0 5.5 %collective-permute-done.17 = bf16[128,256]{1,0:T(8,128)(2,1)S(1)} collective-permute-done((bf16[128,256]{1,0:T(8,128)(2,1)S(1)}, bf16[128,256]{1,0:T(8,128)(2,1)S(1)}, u32[]{:S(2)}, u32[]{:S(2)}) %collective-permute-start.17) | collective-permute-done | bytes 65568 | tf_op jit(solution)/shard_map/ppermute | solution.py:69
  188.0 1.7 collective-permute-start.26
  189.7 2.5 collective-permute-done.18
  194.8 2.4 collective-permute-done.19
  199.4 6.5 %collective-permute-done.20 = bf16[512,256]{1,0:T(8,128)(2,1)S(1)} collective-permute-done((bf16[512,256]{1,0:T(8,128)(2,1)S(1)}, bf16[512,256]{1,0:T(8,128)(2,1)S(1)}, u32[]{:S(2)}, u32[]{:S(2)}) %collective-permute-start.20) | collective-permute-done | bytes 262176 | tf_op jit(solution)/shard_map/ppermute | solution.py:69
  208.5 6.8 %collective-permute-done.21 = bf16[1024,256]{1,0:T(8,128)(2,1)S(1)} collective-permute-done((bf16[1024,256]{1,0:T(8,128)(2,1)S(1)}, bf16[1024,256]{1,0:T(8,128)(2,1)S(1)}, u32[]{:S(2)}, u32[]{:S(2)}) %collective-permute-start.21) | collective-permute-done | bytes 524320 | tf_op jit(solution)/shard_map/ppermute | solution.py:69
  218.2 4.3 %collective-permute-done.30 = bf16[4096,256]{1,0:T(8,128)(2,1)} collective-permute-done((bf16[4096,256]{1,0:T(8,128)(2,1)S(1)}, bf16[4096,256]{1,0:T(8,128)(2,1)}, u32[]{:S(2)}, u32[]{:S(2)}) %collective-permute-start.30) | collective-permute-done | bytes 2097184 | tf_op jit(solution)/shard_map/ppermute | solution.py:69
  222.4 8.3 %broadcast_select_fusion.1 = (bf16[4096,256]{1,0:T(8,128)(2,1)S(1)}, bf16[4096,256]{1,0:T(8,128)(2,1)}) fusion(bf16[4096,256]{1,0:T(8,128)(2,1)} %collective-permute-done.30, pred[]{:T(512)S(6)} %eq.56, bf16[1024,256]{1,0:T(8,128)(2,1)} %copy-done.2, bf16[1024,256]{1,0:T(8,128)(2,1)} %copy-done.1, bf16[1024,256]{1,0:T(8,128)(2,1)S(1)} %get-tuple-element.11, ...), kind=kLoop, calls=%fused_computation.14 | loop fusion | flops 10485760 | bytes 8388609 | tf_op jit(solution)/shard_map/jit(_where)/select_n | solution.py:91
  230.7 20.9 %fusion.1 = bf16[1,1024,8192]{2,1,0:T(8,128)(2,1)} fusion(bf16[1024,256]{1,0:T(8,128)(2,1)} %copy-done.3, bf16[4096,256]{1,0:T(8,128)(2,1)} %get-tuple-element.3, bf16[4096,256]{1,0:T(8,128)(2,1)S(1)} %get-tuple-element.2, bf16[1,1024,8192]{2,1,0:T(8,128)(2,1)} %param.4, bf16[1,1024,8192]{2,1,0:T(8,128)(2,1)} %param.3), kind=kOutput, calls=%fused_computation.3 | convolution fusion | flops 4362076160 | bytes 55050240 | tf_op jit(solution)/shard_map/dot_general | solution.py:136
  (102 shorter events, 44.9 us)
Async XLA Ops:
  1.7 9.3 %collective-permute-start = (bf16[1,1,1,512,256]{4,3,2,1,0:T(8,128)(2,1)S(1)}, bf16[1,1,1,512,256]{4,3,2,1,0:T(8,128)(2,1)S(1)}, u32[]{:S(2)}, u32[]{:S(2)}) collective-permute-start(bf16[1,1,1,512,256]{4,3,2,1,0:T(8,128)(2,1)S(1)} %get-tuple-element.30), channel_id=1, source_target_pairs={{0,2},{1,3},{2,0},{3,1},{4,6},{5,7},{6,4},{7,5},{8,10},{9,11},{10,... | collective-permute-start | bytes 786440 | tf_op jit(solution)/shard_map/ppermute | solution.py:69
  4.7 7.8 %collective-permute-start.3 = (bf16[1,1,1,512,256]{4,3,2,1,0:T(8,128)(2,1)S(1)}, bf16[1,1,1,512,256]{4,3,2,1,0:T(8,128)(2,1)S(1)}, u32[]{:S(2)}, u32[]{:S(2)}) collective-permute-start(bf16[1,1,1,512,256]{4,3,2,1,0:T(8,128)(2,1)S(1)} %get-tuple-element.31), channel_id=1, source_target_pairs={{0,4},{1,5},{2,6},{3,7},{4,0},{5,1},{6,2},{7,3},{8,12},{9,13},{10,... | collective-permute-start | bytes 786440 | tf_op jit(solution)/shard_map/ppermute | solution.py:69
  13.6 12.5 %collective-permute-start.1 = (bf16[1,2,1,512,256]{4,3,2,1,0:T(8,128)(2,1)S(1)}, bf16[1,2,1,512,256]{4,3,2,1,0:T(8,128)(2,1)S(1)}, u32[]{:S(2)}, u32[]{:S(2)}) collective-permute-start(bf16[1,2,1,512,256]{4,3,2,1,0:T(8,128)(2,1)S(1)} %pad_maximum_fusion.8), channel_id=1, source_target_pairs={{0,4},{1,5},{2,6},{3,7},{4,0},{5,1},{6,2},{7,3},{8,12},{9,13},{10,... | collective-permute-start | bytes 1572872 | tf_op jit(solution)/shard_map/ppermute | solution.py:69
  15.3 12.3 %collective-permute-start.4 = (bf16[2,1,1,512,256]{4,3,2,1,0:T(8,128)(2,1)S(1)}, bf16[2,1,1,512,256]{4,3,2,1,0:T(8,128)(2,1)S(1)}, u32[]{:S(2)}, u32[]{:S(2)}) collective-permute-start(bf16[2,1,1,512,256]{4,3,2,1,0:T(8,128)(2,1)S(1)} %pad_maximum_fusion.9), channel_id=1, source_target_pairs={{0,2},{1,3},{2,0},{3,1},{4,6},{5,7},{6,4},{7,5},{8,10},{9,11},{10,... | collective-permute-start | bytes 1572872 | tf_op jit(solution)/shard_map/ppermute | solution.py:69
  27.3 2.9 %collective-permute-start.2 = (bf16[2,2,1,512,256]{4,3,2,1,0:T(8,128)(2,1)}, bf16[2,2,1,512,256]{4,3,2,1,0:T(8,128)(2,1)S(1)}, u32[]{:S(2)}, u32[]{:S(2)}) collective-permute-start(bf16[2,2,1,512,256]{4,3,2,1,0:T(8,128)(2,1)} %pad_maximum_fusion.6), channel_id=1, source_target_pairs={{0,1},{1,0},{2,3},{3,2},{4,5},{5,4},{6,7},{7,6},{8,9},{9,8},{10,11... | collective-permute-start | bytes 3145736 | tf_op jit(solution)/shard_map/ppermute | solution.py:69
  28.7 3.1 %collective-permute-start.5 = (bf16[2,2,1,512,256]{4,3,2,1,0:T(8,128)(2,1)}, bf16[2,2,1,512,256]{4,3,2,1,0:T(8,128)(2,1)}, u32[]{:S(2)}, u32[]{:S(2)}) collective-permute-start(bf16[2,2,1,512,256]{4,3,2,1,0:T(8,128)(2,1)} %pad_maximum_fusion.7), channel_id=1, source_target_pairs={{0,1},{1,0},{2,3},{3,2},{4,5},{5,4},{6,7},{7,6},{8,9},{9,8},{10,11... | collective-permute-start | bytes 3145736 | tf_op jit(solution)/shard_map/ppermute | solution.py:69
  50.4 8.4 %collective-permute-start.6 = (bf16[512,256]{1,0:T(8,128)(2,1)S(1)}, bf16[512,256]{1,0:T(8,128)(2,1)S(1)}, u32[]{:S(2)}, u32[]{:S(2)}) collective-permute-start(bf16[512,256]{1,0:T(8,128)(2,1)S(1)} %dynamic-slice_convert_fusion.5), channel_id=1, source_target_pairs={{0,8},{8,0},{16,24},{24,16},{1,9},{9,1},{17,25},{25,17},{2,10},{10... | collective-permute-start | bytes 786440 | tf_op jit(solution)/shard_map/ppermute | solution.py:69
  58.9 8.5 %collective-permute-start.7 = (bf16[256,256]{1,0:T(8,128)(2,1)S(1)}, bf16[256,256]{1,0:T(8,128)(2,1)S(1)}, u32[]{:S(2)}, u32[]{:S(2)}) collective-permute-start(bf16[256,256]{1,0:T(8,128)(2,1)S(1)} %dynamic-slice_convert_fusion.8), channel_id=1, source_target_pairs={{0,16},{8,24},{16,0},{24,8},{1,17},{9,25},{17,1},{25,9},{2,18},{10... | collective-permute-start | bytes 393224 | tf_op jit(solution)/shard_map/ppermute | solution.py:69
  67.5 8.5 %collective-permute-start.8 = (bf16[256,256]{1,0:T(8,128)(2,1)S(1)}, bf16[256,256]{1,0:T(8,128)(2,1)S(1)}, u32[]{:S(2)}, u32[]{:S(2)}) collective-permute-start(bf16[256,256]{1,0:T(8,128)(2,1)S(1)} %add_convert_fusion.1), channel_id=1, source_target_pairs={{0,16},{8,24},{16,0},{24,8},{1,17},{9,25},{17,1},{25,9},{2,18},{10... | collective-permute-start | bytes 393224 | tf_op jit(solution)/shard_map/ppermute | solution.py:69
  76.1 6.4 %collective-permute-start.9 = (bf16[512,256]{1,0:T(8,128)(2,1)S(1)}, bf16[512,256]{1,0:T(8,128)(2,1)S(1)}, u32[]{:S(2)}, u32[]{:S(2)}) collective-permute-start(bf16[512,256]{1,0:T(8,128)(2,1)S(1)} %pad_maximum_fusion.15), channel_id=1, source_target_pairs={{0,8},{8,0},{16,24},{24,16},{1,9},{9,1},{17,25},{25,17},{2,10},{10... | collective-permute-start | bytes 786440 | tf_op jit(solution)/shard_map/ppermute | solution.py:69
  82.9 1.6 collective-permute-start.10
  84.6 8.4 %collective-permute-start.11 = (f32[256,256]{1,0:T(8,128)S(1)}, f32[256,256]{1,0:T(8,128)S(1)}, u32[]{:S(2)}, u32[]{:S(2)}) collective-permute-start(f32[256,256]{1,0:T(8,128)S(1)} %add.164), channel_id=1, source_target_pairs={{0,2},{1,3},{2,0},{3,1},{4,6},{5,7},{6,4},{7,5},{8,10},{9,11},{10,... | collective-permute-start | bytes 786440 | tf_op jit(solution)/shard_map/ppermute | solution.py:69
  93.0 7.6 %collective-permute-start.12 = (f32[256,256]{1,0:T(8,128)S(1)}, f32[256,256]{1,0:T(8,128)S(1)}, u32[]{:S(2)}, u32[]{:S(2)}) collective-permute-start(f32[256,256]{1,0:T(8,128)S(1)} %add.165), channel_id=1, source_target_pairs={{0,4},{1,5},{2,6},{3,7},{4,0},{5,1},{6,2},{7,3},{8,12},{9,13},{10,... | collective-permute-start | bytes 786440 | tf_op jit(solution)/shard_map/ppermute | solution.py:69
  114.6 22.2 %copy-start.3 = (bf16[1024,256]{1,0:T(8,128)(2,1)}, bf16[1024,256]{1,0:T(8,128)(2,1)S(1)}, u32[]{:S(2)}) copy-start(bf16[1024,256]{1,0:T(8,128)(2,1)S(1)} %convolution_convert_fusion) | copy-start | bytes 1572868
  139.2 4.4 %collective-permute-start.13 = (bf16[4096,256]{1,0:T(8,128)(2,1)S(1)}, bf16[4096,256]{1,0:T(8,128)(2,1)}, u32[]{:S(2)}, u32[]{:S(2)}) collective-permute-start(bf16[4096,256]{1,0:T(8,128)(2,1)S(1)} %dynamic-slice_convert_fusion), channel_id=1, source_target_pairs={{0,1},{1,0},{2,3},{3,2},{4,5},{5,4},{6,7},{7,6},{8,9},{9,8},{10,11... | collective-permute-start | bytes 6291464 | tf_op jit(solution)/shard_map/ppermute | solution.py:69
  148.4 14.1 %collective-permute-start.14 = (bf16[1024,256]{1,0:T(8,128)(2,1)S(1)}, bf16[1024,256]{1,0:T(8,128)(2,1)}, u32[]{:S(2)}, u32[]{:S(2)}) collective-permute-start(bf16[1024,256]{1,0:T(8,128)(2,1)S(1)} %dynamic-slice_convert_fusion.2), channel_id=1, source_target_pairs={{0,2},{1,3},{2,0},{3,1},{4,6},{5,7},{6,4},{7,5},{8,10},{9,11},{10,... | collective-permute-start | bytes 1572872 | tf_op jit(solution)/shard_map/ppermute | solution.py:69
  149.1 16.5 %collective-permute-start.22 = (bf16[1024,256]{1,0:T(8,128)(2,1)S(1)}, bf16[1024,256]{1,0:T(8,128)(2,1)}, u32[]{:S(2)}, u32[]{:S(2)}) collective-permute-start(bf16[1024,256]{1,0:T(8,128)(2,1)S(1)} %dynamic-slice_convert_fusion.1), channel_id=1, source_target_pairs={{0,4},{1,5},{2,6},{3,7},{4,0},{5,1},{6,2},{7,3},{8,12},{9,13},{10,... | collective-permute-start | bytes 1572872 | tf_op jit(solution)/shard_map/ppermute | solution.py:69
  164.1 7.6 %collective-permute-start.15 = (bf16[512,256]{1,0:T(8,128)(2,1)S(1)}, bf16[512,256]{1,0:T(8,128)(2,1)S(1)}, u32[]{:S(2)}, u32[]{:S(2)}) collective-permute-start(bf16[512,256]{1,0:T(8,128)(2,1)S(1)} %dynamic-slice_convert_fusion.4), channel_id=1, source_target_pairs={{0,4},{1,5},{2,6},{3,7},{4,0},{5,1},{6,2},{7,3},{8,12},{9,13},{10,... | collective-permute-start | bytes 786440 | tf_op jit(solution)/shard_map/ppermute | solution.py:69
  166.9 7.3 %collective-permute-start.23 = (bf16[512,256]{1,0:T(8,128)(2,1)S(1)}, bf16[512,256]{1,0:T(8,128)(2,1)S(1)}, u32[]{:S(2)}, u32[]{:S(2)}) collective-permute-start(bf16[512,256]{1,0:T(8,128)(2,1)S(1)} %dynamic-slice_convert_fusion.3), channel_id=1, source_target_pairs={{0,2},{1,3},{2,0},{3,1},{4,6},{5,7},{6,4},{7,5},{8,10},{9,11},{10,... | collective-permute-start | bytes 786440 | tf_op jit(solution)/shard_map/ppermute | solution.py:69
  171.8 6.1 %collective-permute-start.16 = (bf16[256,256]{1,0:T(8,128)(2,1)S(1)}, bf16[256,256]{1,0:T(8,128)(2,1)S(1)}, u32[]{:S(2)}, u32[]{:S(2)}) collective-permute-start(bf16[256,256]{1,0:T(8,128)(2,1)S(1)} %dynamic-slice_convert_fusion.7), channel_id=1, source_target_pairs={{0,8},{8,0},{16,24},{24,16},{1,9},{9,1},{17,25},{25,17},{2,10},{10... | collective-permute-start | bytes 393224 | tf_op jit(solution)/shard_map/ppermute | solution.py:69
  174.3 5.7 %collective-permute-start.24 = (bf16[256,256]{1,0:T(8,128)(2,1)S(1)}, bf16[256,256]{1,0:T(8,128)(2,1)S(1)}, u32[]{:S(2)}, u32[]{:S(2)}) collective-permute-start(bf16[256,256]{1,0:T(8,128)(2,1)S(1)} %dynamic-slice_convert_fusion.6), channel_id=1, source_target_pairs={{0,8},{8,0},{16,24},{24,16},{1,9},{9,1},{17,25},{25,17},{2,10},{10... | collective-permute-start | bytes 393224 | tf_op jit(solution)/shard_map/ppermute | solution.py:69
  177.9 8.7 %collective-permute-start.17 = (bf16[128,256]{1,0:T(8,128)(2,1)S(1)}, bf16[128,256]{1,0:T(8,128)(2,1)S(1)}, u32[]{:S(2)}, u32[]{:S(2)}) collective-permute-start(bf16[128,256]{1,0:T(8,128)(2,1)S(1)} %dynamic-slice_convert_fusion.10), channel_id=1, source_target_pairs={{0,16},{8,24},{16,0},{24,8},{1,17},{9,25},{17,1},{25,9},{2,18},{10... | collective-permute-start | bytes 196616 | tf_op jit(solution)/shard_map/ppermute | solution.py:69
  180.1 7.9 %collective-permute-start.25 = (bf16[128,256]{1,0:T(8,128)(2,1)S(1)}, bf16[128,256]{1,0:T(8,128)(2,1)S(1)}, u32[]{:S(2)}, u32[]{:S(2)}) collective-permute-start(bf16[128,256]{1,0:T(8,128)(2,1)S(1)} %dynamic-slice_convert_fusion.9), channel_id=1, source_target_pairs={{0,16},{8,24},{16,0},{24,8},{1,17},{9,25},{17,1},{25,9},{2,18},{10... | collective-permute-start | bytes 196616 | tf_op jit(solution)/shard_map/ppermute | solution.py:69
  186.6 5.6 %collective-permute-start.18 = (bf16[128,256]{1,0:T(8,128)(2,1)S(1)}, bf16[128,256]{1,0:T(8,128)(2,1)S(1)}, u32[]{:S(2)}, u32[]{:S(2)}) collective-permute-start(bf16[128,256]{1,0:T(8,128)(2,1)S(1)} %multiply_convert_fusion.1), channel_id=1, source_target_pairs={{0,16},{8,24},{16,0},{24,8},{1,17},{9,25},{17,1},{25,9},{2,18},{10... | collective-permute-start | bytes 196616 | tf_op jit(solution)/shard_map/ppermute | solution.py:69
  188.0 5.3 %collective-permute-start.26 = (bf16[128,256]{1,0:T(8,128)(2,1)S(1)}, bf16[128,256]{1,0:T(8,128)(2,1)S(1)}, u32[]{:S(2)}, u32[]{:S(2)}) collective-permute-start(bf16[128,256]{1,0:T(8,128)(2,1)S(1)} %multiply_convert_fusion), channel_id=1, source_target_pairs={{0,16},{8,24},{16,0},{24,8},{1,17},{9,25},{17,1},{25,9},{2,18},{10... | collective-permute-start | bytes 196616 | tf_op jit(solution)/shard_map/ppermute | solution.py:69
  192.2 5.0 %collective-permute-start.19 = (bf16[256,256]{1,0:T(8,128)(2,1)S(1)}, bf16[256,256]{1,0:T(8,128)(2,1)S(1)}, u32[]{:S(2)}, u32[]{:S(2)}) collective-permute-start(bf16[256,256]{1,0:T(8,128)(2,1)S(1)} %pad_maximum_fusion.18), channel_id=1, source_target_pairs={{0,8},{8,0},{16,24},{24,16},{1,9},{9,1},{17,25},{25,17},{2,10},{10... | collective-permute-start | bytes 393224 | tf_op jit(solution)/shard_map/ppermute | solution.py:69
  193.3 5.3 %collective-permute-start.27 = (bf16[256,256]{1,0:T(8,128)(2,1)S(1)}, bf16[256,256]{1,0:T(8,128)(2,1)S(1)}, u32[]{:S(2)}, u32[]{:S(2)}) collective-permute-start(bf16[256,256]{1,0:T(8,128)(2,1)S(1)} %pad_maximum_fusion.19), channel_id=1, source_target_pairs={{0,8},{8,0},{16,24},{24,16},{1,9},{9,1},{17,25},{25,17},{2,10},{10... | collective-permute-start | bytes 393224 | tf_op jit(solution)/shard_map/ppermute | solution.py:69
  197.3 8.6 %collective-permute-start.20 = (bf16[512,256]{1,0:T(8,128)(2,1)S(1)}, bf16[512,256]{1,0:T(8,128)(2,1)S(1)}, u32[]{:S(2)}, u32[]{:S(2)}) collective-permute-start(bf16[512,256]{1,0:T(8,128)(2,1)S(1)} %pad_maximum_fusion.16), channel_id=1, source_target_pairs={{0,4},{1,5},{2,6},{3,7},{4,0},{5,1},{6,2},{7,3},{8,12},{9,13},{10,... | collective-permute-start | bytes 786440 | tf_op jit(solution)/shard_map/ppermute | solution.py:69
  198.7 8.9 %collective-permute-start.28 = (bf16[512,256]{1,0:T(8,128)(2,1)S(1)}, bf16[512,256]{1,0:T(8,128)(2,1)S(1)}, u32[]{:S(2)}, u32[]{:S(2)}) collective-permute-start(bf16[512,256]{1,0:T(8,128)(2,1)S(1)} %pad_maximum_fusion.17), channel_id=1, source_target_pairs={{0,2},{1,3},{2,0},{3,1},{4,6},{5,7},{6,4},{7,5},{8,10},{9,11},{10,... | collective-permute-start | bytes 786440 | tf_op jit(solution)/shard_map/ppermute | solution.py:69
  206.0 9.2 %collective-permute-start.21 = (bf16[1024,256]{1,0:T(8,128)(2,1)S(1)}, bf16[1024,256]{1,0:T(8,128)(2,1)S(1)}, u32[]{:S(2)}, u32[]{:S(2)}) collective-permute-start(bf16[1024,256]{1,0:T(8,128)(2,1)S(1)} %pad_maximum_fusion.11), channel_id=1, source_target_pairs={{0,2},{1,3},{2,0},{3,1},{4,6},{5,7},{6,4},{7,5},{8,10},{9,11},{10,... | collective-permute-start | bytes 1572872 | tf_op jit(solution)/shard_map/ppermute | solution.py:69
  207.7 9.2 %collective-permute-start.29 = (bf16[1024,256]{1,0:T(8,128)(2,1)S(1)}, bf16[1024,256]{1,0:T(8,128)(2,1)S(1)}, u32[]{:S(2)}, u32[]{:S(2)}) collective-permute-start(bf16[1024,256]{1,0:T(8,128)(2,1)S(1)} %pad_maximum_fusion.12), channel_id=1, source_target_pairs={{0,4},{1,5},{2,6},{3,7},{4,0},{5,1},{6,2},{7,3},{8,12},{9,13},{10,... | collective-permute-start | bytes 1572872 | tf_op jit(solution)/shard_map/ppermute | solution.py:69
  218.1 4.3 %collective-permute-start.30 = (bf16[4096,256]{1,0:T(8,128)(2,1)S(1)}, bf16[4096,256]{1,0:T(8,128)(2,1)}, u32[]{:S(2)}, u32[]{:S(2)}) collective-permute-start(bf16[4096,256]{1,0:T(8,128)(2,1)S(1)} %pad_maximum_fusion.5), channel_id=1, source_target_pairs={{0,1},{1,0},{2,3},{3,2},{4,5},{5,4},{6,7},{7,6},{8,9},{9,8},{10,11... | collective-permute-start | bytes 6291464 | tf_op jit(solution)/shard_map/ppermute | solution.py:69
  (3 other events, 3.1 us)

commit v2 on v1

--- a/solution.py
+++ b/solution.py
@@ -8,7 +8,7 @@
 from jax.sharding import PartitionSpec as P
 
 F32, BF16 = jnp.float32, jnp.bfloat16
-PANEL, GROUP = 32, 4
+PANEL, GROUP, TILE = 32, 4, 512
 
 
 def dot_hi(a, b, dims):
@@ -64,6 +64,49 @@
     )(gram)
 
 
+def term_kernel(left_ref, adjusted_ref, out_ref):
+    product = jnp.dot(left_ref[...], adjusted_ref[...], preferred_element_type=F32)
+    out_ref[...] = product.T
+
+
+def term_of(adjusted, basis):
+    rows, cols = adjusted.shape
+    rank = basis.shape[1]
+    return pl.pallas_call(
+        term_kernel,
+        grid=(cols // TILE,),
+        out_shape=jax.ShapeDtypeStruct((cols, rank), F32),
+        in_specs=[pl.BlockSpec((rank, rows), lambda j: (0, 0)), pl.BlockSpec((rows, TILE), lambda j: (0, j))],
+        out_specs=pl.BlockSpec((TILE, rank), lambda j: (j, 0)),
+        cost_estimate=pl.CostEstimate(flops=2 * rows * cols * rank, bytes_accessed=2 * rows * cols + 4 * cols * rank, transcendentals=0),
+        compiler_params=pltpu.CompilerParams(vmem_limit_bytes=16 * 2**20),
+    )(basis.T, adjusted)
+
+
+def residual_kernel(tiles, mine_ref, basis_ref, held_ref, got_ref, adjusted_ref, out_ref):
+    is_held = (pl.program_id(0) // tiles) == mine_ref[0]
+    factor = jnp.where(is_held, held_ref[...].astype(F32), got_ref[...].astype(F32)).astype(BF16)
+    approx = lax.dot_general(basis_ref[...], factor, (((1,), (1,)), ((), ())), preferred_element_type=F32)
+    out_ref[...] = (adjusted_ref[...].astype(F32) - approx).astype(BF16)
+
+
+def residual(adjusted, basis, held, got, mine):
+    rows, cols = adjusted.shape
+    rank = basis.shape[1]
+    tiles = cols // 2 // TILE
+    half = pl.BlockSpec((TILE, rank), lambda j: (j % tiles, 0))
+    wide = pl.BlockSpec((rows, TILE), lambda j: (0, j))
+    return pl.pallas_call(
+        functools.partial(residual_kernel, tiles),
+        grid=(2 * tiles,),
+        out_shape=jax.ShapeDtypeStruct((rows, cols), BF16),
+        in_specs=[pl.BlockSpec(memory_space=pltpu.SMEM), pl.BlockSpec((rows, rank), lambda j: (0, 0)), half, half, wide],
+        out_specs=wide,
+        cost_estimate=pl.CostEstimate(flops=2 * rows * cols * rank, bytes_accessed=4 * rows * cols, transcendentals=0),
+        compiler_params=pltpu.CompilerParams(vmem_limit_bytes=16 * 2**20),
+    )(mine.reshape(1).astype(jnp.int32), basis, held, got, adjusted)
+
+
 def swap(value, step):
     axis, bit = step
     return lax.ppermute(value, axis, [(i, i ^ bit) for i in range(lax.axis_size(axis))])
@@ -98,22 +141,24 @@
 
 
 def gather_blocks(value, order, steps):
-    value = value.reshape((1,) * len(steps) + value.shape)
     for place in order:
         value = joined(value, steps[place], len(steps) - 1 - place)
-    return value.reshape((-1,) + value.shape[len(steps):])
+    return value
 
 
 def shards(gradient, error, query):
     replicas = lax.axis_size("dp")
     mp, dp = bits("mp"), bits("dp")
     adjusted = (gradient[0].astype(F32) + error[0].astype(F32)).astype(BF16)
-    half = query.shape[0] // 2
-    forth = list(range(1, len(mp))) + [0]
-    back = list(range(len(mp) - 1, 0, -1)) + [0]
-    whole = jnp.concatenate(
-        [gather_blocks(query[:half], forth, mp), gather_blocks(query[half:], back, mp)], axis=1
-    ).reshape(-1, query.shape[1])
+    half, rank = query.shape[0] // 2, query.shape[1]
+    lead = (1,) * len(mp)
+    forth, back = list(range(1, len(mp))), list(range(len(mp) - 1, 0, -1))
+    halves = (
+        gather_blocks(query[:half].reshape(lead + (half, rank)), forth, mp),
+        gather_blocks(query[half:].reshape(lead + (half, rank)), back, mp),
+    )
+    adjusted, halves = lax.optimization_barrier((adjusted, halves))
+    whole = jnp.concatenate([gather_blocks(side, [0], mp) for side in halves], axis=len(mp)).reshape(-1, rank)
     projection = jnp.dot(adjusted, whole, preferred_element_type=F32)
     summed = gather(scatter_sum(projection, dp).astype(BF16), dp)
     gram = lax.dot_general(summed, summed, (((0,), (0,)), ((), ())), preferred_element_type=F32)
@@ -121,7 +166,7 @@
         gram = gram + swap(gram, step)
     inverse = inverse_factor(gram)
     basis = dot_hi(summed.astype(F32), inverse, ((1,), (1,))).astype(BF16)
-    term = lax.dot_general(adjusted, basis, (((0,), (0,)), ((), ())), preferred_element_type=F32)
+    term = term_of(adjusted, basis)
     first = scatter_sum(term, mp[:1])
     cut = first.shape[0] // 2
     one, two = mp[1:] + dp, mp[:0:-1] + dp
@@ -129,12 +174,13 @@
     gathered = [
         gather((scatter_sum(part, steps) / replicas).astype(BF16), steps) for part, steps in parts
     ]
-    factor_half = gather(jnp.concatenate(gathered, axis=0), mp[:1])
-    own = lax.dynamic_slice_in_dim(
-        factor_half, lax.axis_index("mp") * query.shape[0], query.shape[0], 0
-    ).astype(F32)
-    approx = lax.dot_general(basis, factor_half, (((1,), (1,)), ((), ())), preferred_element_type=F32)
-    new_error = (adjusted.astype(F32) - approx).astype(BF16)
+    held = jnp.concatenate(gathered, axis=0)
+    got, mine = swap(held, mp[0]), upper(mp[0])
+    start = lax.axis_index("mp") * query.shape[0]
+    span = held.shape[0]
+    own_rows = [lax.dynamic_slice_in_dim(side, start % span, query.shape[0], 0) for side in (held, got)]
+    own = jnp.where(start // span == mine, own_rows[0], own_rows[1]).astype(F32)
+    new_error = residual(adjusted, basis, held, got, mine)
     return (own, new_error[None])
 
 

time: 254 us -> 238 us (0.937)
  matrix products: 58.4 us -> 5.46 us
  Pallas kernels: 13.3 us -> 39.1 us
  local copies, waits for them, and re-layouts: 6.18 us -> 23.1 us
  waiting for transfers between devices: 122 us -> 107 us
  other arithmetic: 24.9 us -> 31.2 us
  starting transfers between devices: 27.6 us -> 30.5 us
    dot_general x2 -> x0, matrix products: 43.1 us -> none  [the longest x1 22.2 us: shards(): lax.dot_general(adjusted, basis, (((0,), (0,)), ((), ())), preferred_elem...]
    pallas_call x0 -> x2, Pallas kernels: none -> 25.8 us  [the longest x1 15.2 us: residual(): pl.pallas_call(functools.partial(residual_kernel, tiles), grid=(2 * tiles...]
    convert_element_type x1 -> x2, other arithmetic: 1.6 us -> 20.4 us  [the longest x1 18.2 us: shards(): adjusted = (gradient[0].astype(F32) + error[0].astype(F32)).astype(BF16)]
    unnamed x8 -> x10, local copies, waits for them, and re-layouts: 2.13 us -> 20.2 us
    ppermute x31, waiting for transfers between devices: 122 us -> 107 us  [swap(): lax.ppermute(value, axis, [(i, i ^ bit) for i in range(lax.axis_size(axis...]
    dot_general x1, matrix products: 14.3 us -> 4.49 us  [shards(): projection = jnp.dot(adjusted, whole, preferred_element_type=F32)]
    select_n x15, other arithmetic: 11.8 us -> 3.7 us  [joined(): jnp.where(mine, got, value)]
    ppermute x31, starting transfers between devices: 27.6 us -> 30.5 us  [swap(): lax.ppermute(value, axis, [(i, i ^ bit) for i in range(lax.axis_size(axis...]
  transfers between devices with their start and end apart: 31 -> 31, of which waited for: 30 -> 27; matrix products, arithmetic and copies ran while one was open for 2% -> 10% of each run, Pallas kernels for 0% -> 0%
where the time goes in v2:
time: 238 us
  waiting for transfers between devices  107 us (45%)
  Pallas kernels  39.1 us (16%)
  other arithmetic  31.2 us (13%)
  starting transfers between devices  30.5 us (13%)
  local copies, waits for them, and re-layouts  23.1 us (10%)
  matrix products  5.46 us (2%)
    ppermute x31, waiting for transfers between devices, swap(): lax.ppermute(value, axis, [(i, i ^ bit) for i in range(lax.axis_size(axis...  107 us
    ppermute x31, starting transfers between devices, swap(): lax.ppermute(value, axis, [(i, i ^ bit) for i in range(lax.axis_size(axis...  30.5 us
    unnamed x10, local copies, waits for them, and re-layouts  20.2 us
    convert_element_type x1, other arithmetic, shards(): adjusted = (gradient[0].astype(F32) + error[0].astype(F32)).astype(BF16)  18.2 us
    pallas_call x1, Pallas kernels, residual(): pl.pallas_call(functools.partial(residual_kernel, tiles), grid=(2 * tiles...  15.2 us
    pallas_call x1, Pallas kernels, inverse_factor(): pl.pallas_call(inverse_kernel, out_shape=jax.ShapeDtypeStruct((rank, rank...  13.3 us
    pallas_call x1, Pallas kernels, term_of(): pl.pallas_call(term_kernel, grid=(cols // TILE,), out_shape=jax.ShapeDtyp...  10.6 us
    add x8, other arithmetic, scatter_sum(): lax.dynamic_slice_in_dim(value, mine * half, half, 0).astype(F32)  6.08 us
  transfers between devices with their start and end apart: 31, of which 27 were waited for; matrix products, arithmetic and copies ran while one was open for 10% of the time, Pallas kernels for 0%

profile of v2, /device:TPU:0, one launch (start us, length us, event | category | flops | bytes accessed | tf_op | source)
XLA Modules:
  0.0 237.7 jit_solution(17424909764416554132)
XLA Ops:
  1.7 3.0 %collective-permute-start = (bf16[1,1,1,512,256]{4,3,2,1,0:T(8,128)(2,1)S(1)}, bf16[1,1,1,512,256]{4,3,2,1,0:T(8,128)(2,1)S(1)}, u32[]{:S(2)}, u32[]{:S(2)}) collective-permute-start(bf16[1,1,1,512,256]{4,3,2,1,0:T(8,128)(2,1)S(1)} %get-tuple-element.35), channel_id=1, source_target_pairs={{0,2},{1,3},{2,0},{3,1},{4,6},{5,7},{6,4},{7,5},{8,10},{9,11},{10,... | collective-permute-start | bytes 786440 | tf_op jit(solution)/shard_map/ppermute | solution.py:112
  6.2 4.8 %collective-permute-done = bf16[1,1,1,512,256]{4,3,2,1,0:T(8,128)(2,1)S(1)} collective-permute-done((bf16[1,1,1,512,256]{4,3,2,1,0:T(8,128)(2,1)S(1)}, bf16[1,1,1,512,256]{4,3,2,1,0:T(8,128)(2,1)S(1)}, u32[]{:S(2)}, u32[]{:S(2)}) %collective-permute-start) | collective-permute-done | bytes 262176 | tf_op jit(solution)/shard_map/ppermute | solution.py:112
  14.1 1.8 collective-permute-start.1
  15.9 18.2 %fusion.adjusted_ref = bf16[1024,8192]{1,0:T(8,128)(2,1)} fusion(bf16[1,1024,8192]{2,1,0:T(8,128)(2,1)} %param.4, bf16[1,1024,8192]{2,1,0:T(8,128)(2,1)} %param.3), kind=kLoop, calls=%fused_computation.1 | loop fusion | flops 33554432 | bytes 50331648 | tf_op jit(solution)/shard_map/convert_element_type | solution.py:152
  35.1 3.0 %collective-permute-done.4 = bf16[2,2,1,512,256]{4,3,2,1,0:T(8,128)(2,1)} collective-permute-done((bf16[2,2,1,512,256]{4,3,2,1,0:T(8,128)(2,1)S(1)}, bf16[2,2,1,512,256]{4,3,2,1,0:T(8,128)(2,1)}, u32[]{:S(2)}, u32[]{:S(2)}) %collective-permute-start.4) | collective-permute-done | bytes 1048608 | tf_op jit(solution)/shard_map/ppermute | solution.py:112
  40.0 4.1 %copy-done = bf16[1024,8192]{1,0:T(8,128)(2,1)S(1)} copy-done((bf16[1024,8192]{1,0:T(8,128)(2,1)S(1)}, bf16[1024,8192]{1,0:T(8,128)(2,1)}, u32[]{:S(2)}) %copy-start) | copy-done | bytes 16777240
  44.1 4.5 %fusion.5 = f32[1024,256]{1,0:T(8,128)S(1)} fusion(bf16[1024,8192]{1,0:T(8,128)(2,1)S(1)} %copy-done, bf16[8192,256]{1,0:T(8,128)(2,1)S(1)} %bitcast.23), kind=kOutput, calls=%fused_computation.78 | convolution fusion | flops 4294967296 | bytes 22020096 | tf_op jit(solution)/shard_map/dot_general | solution.py:162
  50.3 6.8 %collective-permute-done.6 = bf16[512,256]{1,0:T(8,128)(2,1)S(1)} collective-permute-done((bf16[512,256]{1,0:T(8,128)(2,1)S(1)}, bf16[512,256]{1,0:T(8,128)(2,1)S(1)}, u32[]{:S(2)}, u32[]{:S(2)}) %collective-permute-start.6) | collective-permute-done | bytes 262176 | tf_op jit(solution)/shard_map/ppermute | solution.py:112
  57.2 2.7 %collective-permute-start.7 = (bf16[256,256]{1,0:T(8,128)(2,1)S(1)}, bf16[256,256]{1,0:T(8,128)(2,1)S(1)}, u32[]{:S(2)}, u32[]{:S(2)}) collective-permute-start(bf16[256,256]{1,0:T(8,128)(2,1)S(1)} %dynamic-slice_convert_fusion.8), channel_id=1, source_target_pairs={{0,16},{8,24},{16,0},{24,8},{1,17},{9,25},{17,1},{25,9},{2,18},{10... | collective-permute-start | bytes 393224 | tf_op jit(solution)/shard_map/ppermute | solution.py:112
  59.8 5.8 %collective-permute-done.7 = bf16[256,256]{1,0:T(8,128)(2,1)S(1)} collective-permute-done((bf16[256,256]{1,0:T(8,128)(2,1)S(1)}, bf16[256,256]{1,0:T(8,128)(2,1)S(1)}, u32[]{:S(2)}, u32[]{:S(2)}) %collective-permute-start.7) | collective-permute-done | bytes 131104 | tf_op jit(solution)/shard_map/ppermute | solution.py:112
  65.8 8.4 %collective-permute-done.8 = bf16[256,256]{1,0:T(8,128)(2,1)S(1)} collective-permute-done((bf16[256,256]{1,0:T(8,128)(2,1)S(1)}, bf16[256,256]{1,0:T(8,128)(2,1)S(1)}, u32[]{:S(2)}, u32[]{:S(2)}) %collective-permute-start.8) | collective-permute-done | bytes 131104 | tf_op jit(solution)/shard_map/ppermute | solution.py:112
  74.3 6.4 %collective-permute-done.9 = bf16[512,256]{1,0:T(8,128)(2,1)S(1)} collective-permute-done((bf16[512,256]{1,0:T(8,128)(2,1)S(1)}, bf16[512,256]{1,0:T(8,128)(2,1)S(1)}, u32[]{:S(2)}, u32[]{:S(2)}) %collective-permute-start.9) | collective-permute-done | bytes 262176 | tf_op jit(solution)/shard_map/ppermute | solution.py:112
  84.3 6.9 %collective-permute-done.11 = f32[256,256]{1,0:T(8,128)S(1)} collective-permute-done((f32[256,256]{1,0:T(8,128)S(1)}, f32[256,256]{1,0:T(8,128)S(1)}, u32[]{:S(2)}, u32[]{:S(2)}) %collective-permute-start.11) | collective-permute-done | bytes 262176 | tf_op jit(solution)/shard_map/ppermute | solution.py:112
  91.8 7.0 %collective-permute-done.12 = f32[256,256]{1,0:T(8,128)S(1)} collective-permute-done((f32[256,256]{1,0:T(8,128)S(1)}, f32[256,256]{1,0:T(8,128)S(1)}, u32[]{:S(2)}, u32[]{:S(2)}) %collective-permute-start.12) | collective-permute-done | bytes 262176 | tf_op jit(solution)/shard_map/ppermute | solution.py:112
  98.9 13.3 %shard_map.50 = f32[256,256]{1,0:T(8,128)S(1)} custom-call(f32[256,256]{1,0:T(8,128)S(1)} %add.171.gram_ref), custom_call_target="tpu_custom_call" | custom-call | tf_op jit(solution)/shard_map/pallas_call | solution.py:57
  113.0 5.8 %copy-done.1 = bf16[1024,8192]{1,0:T(8,128)(2,1)S(1)} copy-done((bf16[1024,8192]{1,0:T(8,128)(2,1)S(1)}, bf16[1024,8192]{1,0:T(8,128)(2,1)}, u32[]{:S(2)}) %copy-start.1) | copy-done | bytes 16777240
  118.8 10.6 %shard_map.51 = f32[8192,256]{1,0:T(8,128)S(1)} custom-call(bf16[256,1024]{1,0:T(8,128)(2,1)S(1)} %copy.5.left_ref, bf16[1024,8192]{1,0:T(8,128)(2,1)S(1)} %copy-done.1), custom_call_target="tpu_custom_call" | custom-call | flops 4294967296 | bytes 25165824 | tf_op jit(solution)/shard_map/pallas_call | solution.py:75
  129.4 3.3 %copy-done.3 = f32[8192,256]{1,0:T(8,128)} copy-done((f32[8192,256]{1,0:T(8,128)}, f32[8192,256]{1,0:T(8,128)S(1)}, u32[]{:S(2)}) %copy-start.3) | copy-done | bytes 8388632
  133.0 4.3 %collective-permute-done.13 = bf16[4096,256]{1,0:T(8,128)(2,1)} collective-permute-done((bf16[4096,256]{1,0:T(8,128)(2,1)S(1)}, bf16[4096,256]{1,0:T(8,128)(2,1)}, u32[]{:S(2)}, u32[]{:S(2)}) %collective-permute-start.13) | collective-permute-done | bytes 2097184 | tf_op jit(solution)/shard_map/ppermute | solution.py:112
  137.3 3.2 %convert_add_fusion = f32[4096,256]{1,0:T(8,128)S(1)} fusion(bf16[4096,256]{1,0:T(8,128)(2,1)} %collective-permute-done.13, f32[8192,256]{1,0:T(8,128)} %copy-done.3, s32[]{:T(128)S(6)} %select_n.392), kind=kLoop, calls=%fused_computation.3 | loop fusion | flops 2097152 | bytes 10485764 | tf_op jit(solution)/shard_map/add | solution.py:128
  145.1 11.2 %collective-permute-done.14 = bf16[1024,256]{1,0:T(8,128)(2,1)} collective-permute-done((bf16[1024,256]{1,0:T(8,128)(2,1)S(1)}, bf16[1024,256]{1,0:T(8,128)(2,1)}, u32[]{:S(2)}, u32[]{:S(2)}) %collective-permute-start.14) | collective-permute-done | bytes 524320 | tf_op jit(solution)/shard_map/ppermute | solution.py:112
  161.1 4.3 %collective-permute-done.15 = bf16[512,256]{1,0:T(8,128)(2,1)S(1)} collective-permute-done((bf16[512,256]{1,0:T(8,128)(2,1)S(1)}, bf16[512,256]{1,0:T(8,128)(2,1)S(1)}, u32[]{:S(2)}, u32[]{:S(2)}) %collective-permute-start.15) | collective-permute-done | bytes 262176 | tf_op jit(solution)/shard_map/ppermute | solution.py:112
  167.8 3.0 %collective-permute-done.16 = bf16[256,256]{1,0:T(8,128)(2,1)S(1)} collective-permute-done((bf16[256,256]{1,0:T(8,128)(2,1)S(1)}, bf16[256,256]{1,0:T(8,128)(2,1)S(1)}, u32[]{:S(2)}, u32[]{:S(2)}) %collective-permute-start.16) | collective-permute-done | bytes 131104 | tf_op jit(solution)/shard_map/ppermute | solution.py:112
  174.1 5.4 %collective-permute-done.17 = bf16[128,256]{1,0:T(8,128)(2,1)S(1)} collective-permute-done((bf16[128,256]{1,0:T(8,128)(2,1)S(1)}, bf16[128,256]{1,0:T(8,128)(2,1)S(1)}, u32[]{:S(2)}, u32[]{:S(2)}) %collective-permute-start.17) | collective-permute-done | bytes 65568 | tf_op jit(solution)/shard_map/ppermute | solution.py:112
  182.5 2.5 %collective-permute-done.18 = bf16[128,256]{1,0:T(8,128)(2,1)S(1)} collective-permute-done((bf16[128,256]{1,0:T(8,128)(2,1)S(1)}, bf16[128,256]{1,0:T(8,128)(2,1)S(1)}, u32[]{:S(2)}, u32[]{:S(2)}) %collective-permute-start.18) | collective-permute-done | bytes 65568 | tf_op jit(solution)/shard_map/ppermute | solution.py:112
  187.6 2.5 %collective-permute-done.19 = bf16[256,256]{1,0:T(8,128)(2,1)S(1)} collective-permute-done((bf16[256,256]{1,0:T(8,128)(2,1)S(1)}, bf16[256,256]{1,0:T(8,128)(2,1)S(1)}, u32[]{:S(2)}, u32[]{:S(2)}) %collective-permute-start.19) | collective-permute-done | bytes 131104 | tf_op jit(solution)/shard_map/ppermute | solution.py:112
  193.3 5.4 %collective-permute-done.20 = bf16[512,256]{1,0:T(8,128)(2,1)S(1)} collective-permute-done((bf16[512,256]{1,0:T(8,128)(2,1)S(1)}, bf16[512,256]{1,0:T(8,128)(2,1)S(1)}, u32[]{:S(2)}, u32[]{:S(2)}) %collective-permute-start.20) | collective-permute-done | bytes 262176 | tf_op jit(solution)/shard_map/ppermute | solution.py:112
  202.0 6.1 %collective-permute-done.21 = bf16[1024,256]{1,0:T(8,128)(2,1)S(1)} collective-permute-done((bf16[1024,256]{1,0:T(8,128)(2,1)S(1)}, bf16[1024,256]{1,0:T(8,128)(2,1)S(1)}, u32[]{:S(2)}, u32[]{:S(2)}) %collective-permute-start.21) | collective-permute-done | bytes 524320 | tf_op jit(solution)/shard_map/ppermute | solution.py:112
  210.3 4.2 %collective-permute-done.30.got_ref = bf16[4096,256]{1,0:T(8,128)(2,1)} collective-permute-done((bf16[4096,256]{1,0:T(8,128)(2,1)S(1)}, bf16[4096,256]{1,0:T(8,128)(2,1)}, u32[]{:S(2)}, u32[]{:S(2)}) %collective-permute-start.30) | collective-permute-done | bytes 2097184 | tf_op jit(solution)/shard_map/ppermute | solution.py:112
  214.6 5.8 %copy-done.2 = bf16[1024,8192]{1,0:T(8,128)(2,1)S(1)} copy-done((bf16[1024,8192]{1,0:T(8,128)(2,1)S(1)}, bf16[1024,8192]{1,0:T(8,128)(2,1)}, u32[]{:S(2)}) %copy-start.2) | copy-done | bytes 16777240
  220.4 15.2 %shard_map.52 = bf16[1024,8192]{1,0:T(8,128)(2,1)} custom-call(s32[1]{0:T(128)} %bitcast.5.mine_ref, bf16[1024,256]{1,0:T(8,128)(2,1)S(1)} %convolution_convert_fusion.basis_ref, bf16[4096,256]{1,0:T(8,128)(2,1)S(1)} %pad_maximum_fusion.held_ref, bf16[4096,256]{1,0:T(8,128)(2,1)} %collective-permute-done.30.got_ref, bf16[1024,8192]{1,0:T(8,128)(2,1)S(1)} %copy-done.2), custom_call_target="tpu_custom_call" | custom-call | flops 4294967296 | bytes 33554432 | tf_op jit(solution)/shard_map/pallas_call | solution.py:99
  235.6 2.1 select_convert_fusion
  (103 shorter events, 45.2 us)
Async XLA Ops:
  1.7 9.3 %collective-permute-start = (bf16[1,1,1,512,256]{4,3,2,1,0:T(8,128)(2,1)S(1)}, bf16[1,1,1,512,256]{4,3,2,1,0:T(8,128)(2,1)S(1)}, u32[]{:S(2)}, u32[]{:S(2)}) collective-permute-start(bf16[1,1,1,512,256]{4,3,2,1,0:T(8,128)(2,1)S(1)} %get-tuple-element.35), channel_id=1, source_target_pairs={{0,2},{1,3},{2,0},{3,1},{4,6},{5,7},{6,4},{7,5},{8,10},{9,11},{10,... | collective-permute-start | bytes 786440 | tf_op jit(solution)/shard_map/ppermute | solution.py:112
  4.7 7.8 %collective-permute-start.2 = (bf16[1,1,1,512,256]{4,3,2,1,0:T(8,128)(2,1)S(1)}, bf16[1,1,1,512,256]{4,3,2,1,0:T(8,128)(2,1)S(1)}, u32[]{:S(2)}, u32[]{:S(2)}) collective-permute-start(bf16[1,1,1,512,256]{4,3,2,1,0:T(8,128)(2,1)S(1)} %get-tuple-element.34), channel_id=1, source_target_pairs={{0,4},{1,5},{2,6},{3,7},{4,0},{5,1},{6,2},{7,3},{8,12},{9,13},{10,... | collective-permute-start | bytes 786440 | tf_op jit(solution)/shard_map/ppermute | solution.py:112
  13.6 20.5 %collective-permute-start.3 = (bf16[2,1,1,512,256]{4,3,2,1,0:T(8,128)(2,1)S(1)}, bf16[2,1,1,512,256]{4,3,2,1,0:T(8,128)(2,1)S(1)}, u32[]{:S(2)}, u32[]{:S(2)}) collective-permute-start(bf16[2,1,1,512,256]{4,3,2,1,0:T(8,128)(2,1)S(1)} %pad_maximum_fusion.4), channel_id=1, source_target_pairs={{0,2},{1,3},{2,0},{3,1},{4,6},{5,7},{6,4},{7,5},{8,10},{9,11},{10,... | collective-permute-start | bytes 1572872 | tf_op jit(solution)/shard_map/ppermute | solution.py:112
  14.1 20.1 %collective-permute-start.1 = (bf16[1,2,1,512,256]{4,3,2,1,0:T(8,128)(2,1)S(1)}, bf16[1,2,1,512,256]{4,3,2,1,0:T(8,128)(2,1)S(1)}, u32[]{:S(2)}, u32[]{:S(2)}) collective-permute-start(bf16[1,2,1,512,256]{4,3,2,1,0:T(8,128)(2,1)S(1)} %pad_maximum_fusion.3), channel_id=1, source_target_pairs={{0,4},{1,5},{2,6},{3,7},{4,0},{5,1},{6,2},{7,3},{8,12},{9,13},{10,... | collective-permute-start | bytes 1572872 | tf_op jit(solution)/shard_map/ppermute | solution.py:112
  34.5 3.6 %collective-permute-start.4 = (bf16[2,2,1,512,256]{4,3,2,1,0:T(8,128)(2,1)S(1)}, bf16[2,2,1,512,256]{4,3,2,1,0:T(8,128)(2,1)}, u32[]{:S(2)}, u32[]{:S(2)}) collective-permute-start(bf16[2,2,1,512,256]{4,3,2,1,0:T(8,128)(2,1)S(1)} %get-tuple-element.6), channel_id=1, source_target_pairs={{0,1},{1,0},{2,3},{3,2},{4,5},{5,4},{6,7},{7,6},{8,9},{9,8},{10,11... | collective-permute-start | bytes 3145736 | tf_op jit(solution)/shard_map/ppermute | solution.py:112
  34.6 5.0 %collective-permute-start.5 = (bf16[2,2,1,512,256]{4,3,2,1,0:T(8,128)(2,1)S(1)}, bf16[2,2,1,512,256]{4,3,2,1,0:T(8,128)(2,1)S(1)}, u32[]{:S(2)}, u32[]{:S(2)}) collective-permute-start(bf16[2,2,1,512,256]{4,3,2,1,0:T(8,128)(2,1)S(1)} %get-tuple-element.7), channel_id=1, source_target_pairs={{0,1},{1,0},{2,3},{3,2},{4,5},{5,4},{6,7},{7,6},{8,9},{9,8},{10,11... | collective-permute-start | bytes 3145736 | tf_op jit(solution)/shard_map/ppermute | solution.py:112
  38.0 6.1 %copy-start = (bf16[1024,8192]{1,0:T(8,128)(2,1)S(1)}, bf16[1024,8192]{1,0:T(8,128)(2,1)}, u32[]{:S(2)}) copy-start(bf16[1024,8192]{1,0:T(8,128)(2,1)} %fusion.adjusted_ref) | copy-start | bytes 50331652
  48.7 8.4 %collective-permute-start.6 = (bf16[512,256]{1,0:T(8,128)(2,1)S(1)}, bf16[512,256]{1,0:T(8,128)(2,1)S(1)}, u32[]{:S(2)}, u32[]{:S(2)}) collective-permute-start(bf16[512,256]{1,0:T(8,128)(2,1)S(1)} %dynamic-slice_convert_fusion.5), channel_id=1, source_target_pairs={{0,8},{8,0},{16,24},{24,16},{1,9},{9,1},{17,25},{25,17},{2,10},{10... | collective-permute-start | bytes 786440 | tf_op jit(solution)/shard_map/ppermute | solution.py:112
  57.2 8.5 %collective-permute-start.7 = (bf16[256,256]{1,0:T(8,128)(2,1)S(1)}, bf16[256,256]{1,0:T(8,128)(2,1)S(1)}, u32[]{:S(2)}, u32[]{:S(2)}) collective-permute-start(bf16[256,256]{1,0:T(8,128)(2,1)S(1)} %dynamic-slice_convert_fusion.8), channel_id=1, source_target_pairs={{0,16},{8,24},{16,0},{24,8},{1,17},{9,25},{17,1},{25,9},{2,18},{10... | collective-permute-start | bytes 393224 | tf_op jit(solution)/shard_map/ppermute | solution.py:112
  65.7 8.5 %collective-permute-start.8 = (bf16[256,256]{1,0:T(8,128)(2,1)S(1)}, bf16[256,256]{1,0:T(8,128)(2,1)S(1)}, u32[]{:S(2)}, u32[]{:S(2)}) collective-permute-start(bf16[256,256]{1,0:T(8,128)(2,1)S(1)} %add_convert_fusion.1), channel_id=1, source_target_pairs={{0,16},{8,24},{16,0},{24,8},{1,17},{9,25},{17,1},{25,9},{2,18},{10... | collective-permute-start | bytes 393224 | tf_op jit(solution)/shard_map/ppermute | solution.py:112
  74.3 6.4 %collective-permute-start.9 = (bf16[512,256]{1,0:T(8,128)(2,1)S(1)}, bf16[512,256]{1,0:T(8,128)(2,1)S(1)}, u32[]{:S(2)}, u32[]{:S(2)}) collective-permute-start(bf16[512,256]{1,0:T(8,128)(2,1)S(1)} %pad_maximum_fusion.10), channel_id=1, source_target_pairs={{0,8},{8,0},{16,24},{24,16},{1,9},{9,1},{17,25},{25,17},{2,10},{10... | collective-permute-start | bytes 786440 | tf_op jit(solution)/shard_map/ppermute | solution.py:112
  81.1 1.6 collective-permute-start.10
  82.8 8.4 %collective-permute-start.11 = (f32[256,256]{1,0:T(8,128)S(1)}, f32[256,256]{1,0:T(8,128)S(1)}, u32[]{:S(2)}, u32[]{:S(2)}) collective-permute-start(f32[256,256]{1,0:T(8,128)S(1)} %add.169), channel_id=1, source_target_pairs={{0,2},{1,3},{2,0},{3,1},{4,6},{5,7},{6,4},{7,5},{8,10},{9,11},{10,... | collective-permute-start | bytes 786440 | tf_op jit(solution)/shard_map/ppermute | solution.py:112
  91.2 7.6 %collective-permute-start.12 = (f32[256,256]{1,0:T(8,128)S(1)}, f32[256,256]{1,0:T(8,128)S(1)}, u32[]{:S(2)}, u32[]{:S(2)}) collective-permute-start(f32[256,256]{1,0:T(8,128)S(1)} %add.170), channel_id=1, source_target_pairs={{0,4},{1,5},{2,6},{3,7},{4,0},{5,1},{6,2},{7,3},{8,12},{9,13},{10,... | collective-permute-start | bytes 786440 | tf_op jit(solution)/shard_map/ppermute | solution.py:112
  132.9 4.4 %collective-permute-start.13 = (bf16[4096,256]{1,0:T(8,128)(2,1)S(1)}, bf16[4096,256]{1,0:T(8,128)(2,1)}, u32[]{:S(2)}, u32[]{:S(2)}) collective-permute-start(bf16[4096,256]{1,0:T(8,128)(2,1)S(1)} %dynamic-slice_convert_fusion), channel_id=1, source_target_pairs={{0,1},{1,0},{2,3},{3,2},{4,5},{5,4},{6,7},{7,6},{8,9},{9,8},{10,11... | collective-permute-start | bytes 6291464 | tf_op jit(solution)/shard_map/ppermute | solution.py:112
  142.2 14.1 %collective-permute-start.14 = (bf16[1024,256]{1,0:T(8,128)(2,1)S(1)}, bf16[1024,256]{1,0:T(8,128)(2,1)}, u32[]{:S(2)}, u32[]{:S(2)}) collective-permute-start(bf16[1024,256]{1,0:T(8,128)(2,1)S(1)} %dynamic-slice_convert_fusion.2), channel_id=1, source_target_pairs={{0,2},{1,3},{2,0},{3,1},{4,6},{5,7},{6,4},{7,5},{8,10},{9,11},{10,... | collective-permute-start | bytes 1572872 | tf_op jit(solution)/shard_map/ppermute | solution.py:112
  144.5 14.0 %collective-permute-start.22 = (bf16[1024,256]{1,0:T(8,128)(2,1)}, bf16[1024,256]{1,0:T(8,128)(2,1)}, u32[]{:S(2)}, u32[]{:S(2)}) collective-permute-start(bf16[1024,256]{1,0:T(8,128)(2,1)} %dynamic-slice_convert_fusion.1), channel_id=1, source_target_pairs={{0,4},{1,5},{2,6},{3,7},{4,0},{5,1},{6,2},{7,3},{8,12},{9,13},{10,... | collective-permute-start | bytes 1572872 | tf_op jit(solution)/shard_map/ppermute | solution.py:112
  157.8 7.6 %collective-permute-start.15 = (bf16[512,256]{1,0:T(8,128)(2,1)S(1)}, bf16[512,256]{1,0:T(8,128)(2,1)S(1)}, u32[]{:S(2)}, u32[]{:S(2)}) collective-permute-start(bf16[512,256]{1,0:T(8,128)(2,1)S(1)} %dynamic-slice_convert_fusion.4), channel_id=1, source_target_pairs={{0,4},{1,5},{2,6},{3,7},{4,0},{5,1},{6,2},{7,3},{8,12},{9,13},{10,... | collective-permute-start | bytes 786440 | tf_op jit(solution)/shard_map/ppermute | solution.py:112
  159.7 7.3 %collective-permute-start.23 = (bf16[512,256]{1,0:T(8,128)(2,1)S(1)}, bf16[512,256]{1,0:T(8,128)(2,1)S(1)}, u32[]{:S(2)}, u32[]{:S(2)}) collective-permute-start(bf16[512,256]{1,0:T(8,128)(2,1)S(1)} %dynamic-slice_convert_fusion.3), channel_id=1, source_target_pairs={{0,2},{1,3},{2,0},{3,1},{4,6},{5,7},{6,4},{7,5},{8,10},{9,11},{10,... | collective-permute-start | bytes 786440 | tf_op jit(solution)/shard_map/ppermute | solution.py:112
  165.5 5.3 %collective-permute-start.16 = (bf16[256,256]{1,0:T(8,128)(2,1)S(1)}, bf16[256,256]{1,0:T(8,128)(2,1)S(1)}, u32[]{:S(2)}, u32[]{:S(2)}) collective-permute-start(bf16[256,256]{1,0:T(8,128)(2,1)S(1)} %dynamic-slice_convert_fusion.7), channel_id=1, source_target_pairs={{0,8},{8,0},{16,24},{24,16},{1,9},{9,1},{17,25},{25,17},{2,10},{10... | collective-permute-start | bytes 393224 | tf_op jit(solution)/shard_map/ppermute | solution.py:112
  167.1 5.8 %collective-permute-start.24 = (bf16[256,256]{1,0:T(8,128)(2,1)S(1)}, bf16[256,256]{1,0:T(8,128)(2,1)S(1)}, u32[]{:S(2)}, u32[]{:S(2)}) collective-permute-start(bf16[256,256]{1,0:T(8,128)(2,1)S(1)} %dynamic-slice_convert_fusion.6), channel_id=1, source_target_pairs={{0,8},{8,0},{16,24},{24,16},{1,9},{9,1},{17,25},{25,17},{2,10},{10... | collective-permute-start | bytes 393224 | tf_op jit(solution)/shard_map/ppermute | solution.py:112
  170.8 8.6 %collective-permute-start.17 = (bf16[128,256]{1,0:T(8,128)(2,1)S(1)}, bf16[128,256]{1,0:T(8,128)(2,1)S(1)}, u32[]{:S(2)}, u32[]{:S(2)}) collective-permute-start(bf16[128,256]{1,0:T(8,128)(2,1)S(1)} %dynamic-slice_convert_fusion.10), channel_id=1, source_target_pairs={{0,16},{8,24},{16,0},{24,8},{1,17},{9,25},{17,1},{25,9},{2,18},{10... | collective-permute-start | bytes 196616 | tf_op jit(solution)/shard_map/ppermute | solution.py:112
  172.9 7.9 %collective-permute-start.25 = (bf16[128,256]{1,0:T(8,128)(2,1)S(1)}, bf16[128,256]{1,0:T(8,128)(2,1)S(1)}, u32[]{:S(2)}, u32[]{:S(2)}) collective-permute-start(bf16[128,256]{1,0:T(8,128)(2,1)S(1)} %dynamic-slice_convert_fusion.9), channel_id=1, source_target_pairs={{0,16},{8,24},{16,0},{24,8},{1,17},{9,25},{17,1},{25,9},{2,18},{10... | collective-permute-start | bytes 196616 | tf_op jit(solution)/shard_map/ppermute | solution.py:112
  179.4 5.6 %collective-permute-start.18 = (bf16[128,256]{1,0:T(8,128)(2,1)S(1)}, bf16[128,256]{1,0:T(8,128)(2,1)S(1)}, u32[]{:S(2)}, u32[]{:S(2)}) collective-permute-start(bf16[128,256]{1,0:T(8,128)(2,1)S(1)} %multiply_convert_fusion.1), channel_id=1, source_target_pairs={{0,16},{8,24},{16,0},{24,8},{1,17},{9,25},{17,1},{25,9},{2,18},{10... | collective-permute-start | bytes 196616 | tf_op jit(solution)/shard_map/ppermute | solution.py:112
  180.8 5.3 %collective-permute-start.26 = (bf16[128,256]{1,0:T(8,128)(2,1)S(1)}, bf16[128,256]{1,0:T(8,128)(2,1)S(1)}, u32[]{:S(2)}, u32[]{:S(2)}) collective-permute-start(bf16[128,256]{1,0:T(8,128)(2,1)S(1)} %multiply_convert_fusion), channel_id=1, source_target_pairs={{0,16},{8,24},{16,0},{24,8},{1,17},{9,25},{17,1},{25,9},{2,18},{10... | collective-permute-start | bytes 196616 | tf_op jit(solution)/shard_map/ppermute | solution.py:112
  185.1 5.0 %collective-permute-start.19 = (bf16[256,256]{1,0:T(8,128)(2,1)S(1)}, bf16[256,256]{1,0:T(8,128)(2,1)S(1)}, u32[]{:S(2)}, u32[]{:S(2)}) collective-permute-start(bf16[256,256]{1,0:T(8,128)(2,1)S(1)} %pad_maximum_fusion.13), channel_id=1, source_target_pairs={{0,8},{8,0},{16,24},{24,16},{1,9},{9,1},{17,25},{25,17},{2,10},{10... | collective-permute-start | bytes 393224 | tf_op jit(solution)/shard_map/ppermute | solution.py:112
  186.2 5.4 %collective-permute-start.27 = (bf16[256,256]{1,0:T(8,128)(2,1)S(1)}, bf16[256,256]{1,0:T(8,128)(2,1)S(1)}, u32[]{:S(2)}, u32[]{:S(2)}) collective-permute-start(bf16[256,256]{1,0:T(8,128)(2,1)S(1)} %pad_maximum_fusion.14), channel_id=1, source_target_pairs={{0,8},{8,0},{16,24},{24,16},{1,9},{9,1},{17,25},{25,17},{2,10},{10... | collective-permute-start | bytes 393224 | tf_op jit(solution)/shard_map/ppermute | solution.py:112
  190.2 8.5 %collective-permute-start.20 = (bf16[512,256]{1,0:T(8,128)(2,1)S(1)}, bf16[512,256]{1,0:T(8,128)(2,1)S(1)}, u32[]{:S(2)}, u32[]{:S(2)}) collective-permute-start(bf16[512,256]{1,0:T(8,128)(2,1)S(1)} %pad_maximum_fusion.11), channel_id=1, source_target_pairs={{0,4},{1,5},{2,6},{3,7},{4,0},{5,1},{6,2},{7,3},{8,12},{9,13},{10,... | collective-permute-start | bytes 786440 | tf_op jit(solution)/shard_map/ppermute | solution.py:112
  191.7 8.8 %collective-permute-start.28 = (bf16[512,256]{1,0:T(8,128)(2,1)S(1)}, bf16[512,256]{1,0:T(8,128)(2,1)S(1)}, u32[]{:S(2)}, u32[]{:S(2)}) collective-permute-start(bf16[512,256]{1,0:T(8,128)(2,1)S(1)} %pad_maximum_fusion.12), channel_id=1, source_target_pairs={{0,2},{1,3},{2,0},{3,1},{4,6},{5,7},{6,4},{7,5},{8,10},{9,11},{10,... | collective-permute-start | bytes 786440 | tf_op jit(solution)/shard_map/ppermute | solution.py:112
  198.8 9.2 %collective-permute-start.21 = (bf16[1024,256]{1,0:T(8,128)(2,1)S(1)}, bf16[1024,256]{1,0:T(8,128)(2,1)S(1)}, u32[]{:S(2)}, u32[]{:S(2)}) collective-permute-start(bf16[1024,256]{1,0:T(8,128)(2,1)S(1)} %pad_maximum_fusion.6), channel_id=1, source_target_pairs={{0,2},{1,3},{2,0},{3,1},{4,6},{5,7},{6,4},{7,5},{8,10},{9,11},{10,... | collective-permute-start | bytes 1572872 | tf_op jit(solution)/shard_map/ppermute | solution.py:112
  200.6 9.2 %collective-permute-start.29 = (bf16[1024,256]{1,0:T(8,128)(2,1)S(1)}, bf16[1024,256]{1,0:T(8,128)(2,1)S(1)}, u32[]{:S(2)}, u32[]{:S(2)}) collective-permute-start(bf16[1024,256]{1,0:T(8,128)(2,1)S(1)} %pad_maximum_fusion.7), channel_id=1, source_target_pairs={{0,4},{1,5},{2,6},{3,7},{4,0},{5,1},{6,2},{7,3},{8,12},{9,13},{10,... | collective-permute-start | bytes 1572872 | tf_op jit(solution)/shard_map/ppermute | solution.py:112
  210.2 4.4 %collective-permute-start.30 = (bf16[4096,256]{1,0:T(8,128)(2,1)S(1)}, bf16[4096,256]{1,0:T(8,128)(2,1)}, u32[]{:S(2)}, u32[]{:S(2)}) collective-permute-start(bf16[4096,256]{1,0:T(8,128)(2,1)S(1)} %pad_maximum_fusion.held_ref), channel_id=1, source_target_pairs={{0,1},{1,0},{2,3},{3,2},{4,5},{5,4},{6,7},{7,6},{8,9},{9,8},{10,11... | collective-permute-start | bytes 6291464 | tf_op jit(solution)/shard_map/ppermute | solution.py:112
  (4 other events, 16.2 us)

commit v3 on v2

--- a/solution.py
+++ b/solution.py
@@ -79,7 +79,7 @@
         in_specs=[pl.BlockSpec((rank, rows), lambda j: (0, 0)), pl.BlockSpec((rows, TILE), lambda j: (0, j))],
         out_specs=pl.BlockSpec((TILE, rank), lambda j: (j, 0)),
         cost_estimate=pl.CostEstimate(flops=2 * rows * cols * rank, bytes_accessed=2 * rows * cols + 4 * cols * rank, transcendentals=0),
-        compiler_params=pltpu.CompilerParams(vmem_limit_bytes=16 * 2**20),
+        compiler_params=pltpu.CompilerParams(vmem_limit_bytes=49 * 2**20),
     )(basis.T, adjusted)
 
 
@@ -103,7 +103,7 @@
         in_specs=[pl.BlockSpec(memory_space=pltpu.SMEM), pl.BlockSpec((rows, rank), lambda j: (0, 0)), half, half, wide],
         out_specs=wide,
         cost_estimate=pl.CostEstimate(flops=2 * rows * cols * rank, bytes_accessed=4 * rows * cols, transcendentals=0),
-        compiler_params=pltpu.CompilerParams(vmem_limit_bytes=16 * 2**20),
+        compiler_params=pltpu.CompilerParams(vmem_limit_bytes=49 * 2**20),
     )(mine.reshape(1).astype(jnp.int32), basis, held, got, adjusted)
 
 

time: 238 us -> 239 us (level)
  Pallas kernels: 39.1 us -> 52.3 us
  local copies, waits for them, and re-layouts: 23.1 us -> 10.4 us
    unnamed x10 -> x4, local copies, waits for them, and re-layouts: 20.2 us -> 5.39 us
    pallas_call x1, Pallas kernels: 10.6 us -> 17.9 us  [term_of(): pl.pallas_call(term_kernel, grid=(cols // TILE,), out_shape=jax.ShapeDtyp...]
    pallas_call x1, Pallas kernels: 15.2 us -> 21.1 us  [residual(): pl.pallas_call(functools.partial(residual_kernel, tiles), grid=(2 * tiles...]
where the time goes in v3:
time: 239 us; the launch traced here: 238 us
  waiting for transfers between devices  107 us (45%)
  Pallas kernels  52.3 us (22%)
  other arithmetic  31.2 us (13%)
  starting transfers between devices  30.6 us (13%)
  local copies, waits for them, and re-layouts  10.4 us (4%)
  matrix products  5.46 us (2%)
    ppermute x31, waiting for transfers between devices, swap(): lax.ppermute(value, axis, [(i, i ^ bit) for i in range(lax.axis_size(axis...  107 us
    ppermute x31, starting transfers between devices, swap(): lax.ppermute(value, axis, [(i, i ^ bit) for i in range(lax.axis_size(axis...  30.6 us
    pallas_call x1, Pallas kernels, residual(): pl.pallas_call(functools.partial(residual_kernel, tiles), grid=(2 * tiles...  21.1 us
    convert_element_type x1, other arithmetic, shards(): adjusted = (gradient[0].astype(F32) + error[0].astype(F32)).astype(BF16)  18.2 us
    pallas_call x1, Pallas kernels, term_of(): pl.pallas_call(term_kernel, grid=(cols // TILE,), out_shape=jax.ShapeDtyp...  17.9 us
    pallas_call x1, Pallas kernels, inverse_factor(): pl.pallas_call(inverse_kernel, out_shape=jax.ShapeDtypeStruct((rank, rank...  13.3 us
    add x8, other arithmetic, scatter_sum(): lax.dynamic_slice_in_dim(value, mine * half, half, 0).astype(F32)  6.08 us
    unnamed x4, local copies, waits for them, and re-layouts  5.39 us
  transfers between devices with their start and end apart: 31, of which 27 were waited for; matrix products, arithmetic and copies ran while one was open for 10% of the time, Pallas kernels for 0%

profile of v3, /device:TPU:0, one launch (start us, length us, event | category | flops | bytes accessed | tf_op | source)
XLA Modules:
  0.0 238.2 jit_solution(2055894434029315221)
XLA Ops:
  1.7 3.0 %collective-permute-start = (bf16[1,1,1,512,256]{4,3,2,1,0:T(8,128)(2,1)S(1)}, bf16[1,1,1,512,256]{4,3,2,1,0:T(8,128)(2,1)S(1)}, u32[]{:S(2)}, u32[]{:S(2)}) collective-permute-start(bf16[1,1,1,512,256]{4,3,2,1,0:T(8,128)(2,1)S(1)} %get-tuple-element.35), channel_id=1, source_target_pairs={{0,2},{1,3},{2,0},{3,1},{4,6},{5,7},{6,4},{7,5},{8,10},{9,11},{10,... | collective-permute-start | bytes 786440 | tf_op jit(solution)/shard_map/ppermute | solution.py:112
  6.2 4.8 %collective-permute-done = bf16[1,1,1,512,256]{4,3,2,1,0:T(8,128)(2,1)S(1)} collective-permute-done((bf16[1,1,1,512,256]{4,3,2,1,0:T(8,128)(2,1)S(1)}, bf16[1,1,1,512,256]{4,3,2,1,0:T(8,128)(2,1)S(1)}, u32[]{:S(2)}, u32[]{:S(2)}) %collective-permute-start) | collective-permute-done | bytes 262176 | tf_op jit(solution)/shard_map/ppermute | solution.py:112
  14.1 1.8 collective-permute-start.1
  15.9 18.2 %fusion.adjusted_ref = bf16[1024,8192]{1,0:T(8,128)(2,1)} fusion(bf16[1,1024,8192]{2,1,0:T(8,128)(2,1)} %param.4, bf16[1,1024,8192]{2,1,0:T(8,128)(2,1)} %param.3), kind=kLoop, calls=%fused_computation.1 | loop fusion | flops 33554432 | bytes 50331648 | tf_op jit(solution)/shard_map/convert_element_type | solution.py:152
  35.0 3.0 %collective-permute-done.4 = bf16[2,2,1,512,256]{4,3,2,1,0:T(8,128)(2,1)} collective-permute-done((bf16[2,2,1,512,256]{4,3,2,1,0:T(8,128)(2,1)S(1)}, bf16[2,2,1,512,256]{4,3,2,1,0:T(8,128)(2,1)}, u32[]{:S(2)}, u32[]{:S(2)}) %collective-permute-start.4) | collective-permute-done | bytes 1048608 | tf_op jit(solution)/shard_map/ppermute | solution.py:112
  40.0 4.1 %copy-done = bf16[1024,8192]{1,0:T(8,128)(2,1)S(1)} copy-done((bf16[1024,8192]{1,0:T(8,128)(2,1)S(1)}, bf16[1024,8192]{1,0:T(8,128)(2,1)}, u32[]{:S(2)}) %copy-start) | copy-done | bytes 16777240
  44.1 4.5 %fusion.5 = f32[1024,256]{1,0:T(8,128)S(1)} fusion(bf16[1024,8192]{1,0:T(8,128)(2,1)S(1)} %copy-done, bf16[8192,256]{1,0:T(8,128)(2,1)S(1)} %bitcast.23), kind=kOutput, calls=%fused_computation.78 | convolution fusion | flops 4294967296 | bytes 22020096 | tf_op jit(solution)/shard_map/dot_general | solution.py:162
  48.6 1.6 collective-permute-start.6
  50.3 6.8 %collective-permute-done.6 = bf16[512,256]{1,0:T(8,128)(2,1)S(1)} collective-permute-done((bf16[512,256]{1,0:T(8,128)(2,1)S(1)}, bf16[512,256]{1,0:T(8,128)(2,1)S(1)}, u32[]{:S(2)}, u32[]{:S(2)}) %collective-permute-start.6) | collective-permute-done | bytes 262176 | tf_op jit(solution)/shard_map/ppermute | solution.py:112
  57.1 2.7 %collective-permute-start.7 = (bf16[256,256]{1,0:T(8,128)(2,1)S(1)}, bf16[256,256]{1,0:T(8,128)(2,1)S(1)}, u32[]{:S(2)}, u32[]{:S(2)}) collective-permute-start(bf16[256,256]{1,0:T(8,128)(2,1)S(1)} %dynamic-slice_convert_fusion.8), channel_id=1, source_target_pairs={{0,16},{8,24},{16,0},{24,8},{1,17},{9,25},{17,1},{25,9},{2,18},{10... | collective-permute-start | bytes 393224 | tf_op jit(solution)/shard_map/ppermute | solution.py:112
  59.8 5.8 %collective-permute-done.7 = bf16[256,256]{1,0:T(8,128)(2,1)S(1)} collective-permute-done((bf16[256,256]{1,0:T(8,128)(2,1)S(1)}, bf16[256,256]{1,0:T(8,128)(2,1)S(1)}, u32[]{:S(2)}, u32[]{:S(2)}) %collective-permute-start.7) | collective-permute-done | bytes 131104 | tf_op jit(solution)/shard_map/ppermute | solution.py:112
  65.8 8.4 %collective-permute-done.8 = bf16[256,256]{1,0:T(8,128)(2,1)S(1)} collective-permute-done((bf16[256,256]{1,0:T(8,128)(2,1)S(1)}, bf16[256,256]{1,0:T(8,128)(2,1)S(1)}, u32[]{:S(2)}, u32[]{:S(2)}) %collective-permute-start.8) | collective-permute-done | bytes 131104 | tf_op jit(solution)/shard_map/ppermute | solution.py:112
  74.3 6.4 %collective-permute-done.9 = bf16[512,256]{1,0:T(8,128)(2,1)S(1)} collective-permute-done((bf16[512,256]{1,0:T(8,128)(2,1)S(1)}, bf16[512,256]{1,0:T(8,128)(2,1)S(1)}, u32[]{:S(2)}, u32[]{:S(2)}) %collective-permute-start.9) | collective-permute-done | bytes 262176 | tf_op jit(solution)/shard_map/ppermute | solution.py:112
  84.3 6.9 %collective-permute-done.11 = f32[256,256]{1,0:T(8,128)S(1)} collective-permute-done((f32[256,256]{1,0:T(8,128)S(1)}, f32[256,256]{1,0:T(8,128)S(1)}, u32[]{:S(2)}, u32[]{:S(2)}) %collective-permute-start.11) | collective-permute-done | bytes 262176 | tf_op jit(solution)/shard_map/ppermute | solution.py:112
  91.8 7.0 %collective-permute-done.12 = f32[256,256]{1,0:T(8,128)S(1)} collective-permute-done((f32[256,256]{1,0:T(8,128)S(1)}, f32[256,256]{1,0:T(8,128)S(1)}, u32[]{:S(2)}, u32[]{:S(2)}) %collective-permute-start.12) | collective-permute-done | bytes 262176 | tf_op jit(solution)/shard_map/ppermute | solution.py:112
  98.8 13.3 %shard_map.50 = f32[256,256]{1,0:T(8,128)S(1)} custom-call(f32[256,256]{1,0:T(8,128)S(1)} %add.171.gram_ref), custom_call_target="tpu_custom_call" | custom-call | tf_op jit(solution)/shard_map/pallas_call | solution.py:57
  113.0 17.9 %shard_map.51 = f32[8192,256]{1,0:T(8,128)} custom-call(bf16[256,1024]{1,0:T(8,128)(2,1)S(1)} %copy.5.left_ref, bf16[1024,8192]{1,0:T(8,128)(2,1)} %fusion.adjusted_ref), custom_call_target="tpu_custom_call" | custom-call | flops 4294967296 | bytes 25165824 | tf_op jit(solution)/shard_map/pallas_call | solution.py:75
  130.9 2.4 %dynamic-slice_convert_fusion = bf16[4096,256]{1,0:T(8,128)(2,1)S(1)} fusion(f32[8192,256]{1,0:T(8,128)} %shard_map.51, s32[]{:T(128)S(6)} %select_n.393), kind=kLoop, calls=%fused_computation.4 | loop fusion | bytes 4194308 | tf_op jit(solution)/shard_map/convert_element_type | solution.py:126
  133.4 4.3 %collective-permute-done.13 = bf16[4096,256]{1,0:T(8,128)(2,1)} collective-permute-done((bf16[4096,256]{1,0:T(8,128)(2,1)S(1)}, bf16[4096,256]{1,0:T(8,128)(2,1)}, u32[]{:S(2)}, u32[]{:S(2)}) %collective-permute-start.13) | collective-permute-done | bytes 2097184 | tf_op jit(solution)/shard_map/ppermute | solution.py:112
  137.6 3.2 %convert_add_fusion = f32[4096,256]{1,0:T(8,128)S(1)} fusion(bf16[4096,256]{1,0:T(8,128)(2,1)} %collective-permute-done.13, f32[8192,256]{1,0:T(8,128)} %shard_map.51, s32[]{:T(128)S(6)} %select_n.392), kind=kLoop, calls=%fused_computation.3 | loop fusion | flops 2097152 | bytes 10485764 | tf_op jit(solution)/shard_map/add | solution.py:128
  145.4 11.2 %collective-permute-done.14 = bf16[1024,256]{1,0:T(8,128)(2,1)} collective-permute-done((bf16[1024,256]{1,0:T(8,128)(2,1)S(1)}, bf16[1024,256]{1,0:T(8,128)(2,1)}, u32[]{:S(2)}, u32[]{:S(2)}) %collective-permute-start.14) | collective-permute-done | bytes 524320 | tf_op jit(solution)/shard_map/ppermute | solution.py:112
  161.5 4.3 %collective-permute-done.15 = bf16[512,256]{1,0:T(8,128)(2,1)S(1)} collective-permute-done((bf16[512,256]{1,0:T(8,128)(2,1)S(1)}, bf16[512,256]{1,0:T(8,128)(2,1)S(1)}, u32[]{:S(2)}, u32[]{:S(2)}) %collective-permute-start.15) | collective-permute-done | bytes 262176 | tf_op jit(solution)/shard_map/ppermute | solution.py:112
  168.1 3.0 %collective-permute-done.16 = bf16[256,256]{1,0:T(8,128)(2,1)S(1)} collective-permute-done((bf16[256,256]{1,0:T(8,128)(2,1)S(1)}, bf16[256,256]{1,0:T(8,128)(2,1)S(1)}, u32[]{:S(2)}, u32[]{:S(2)}) %collective-permute-start.16) | collective-permute-done | bytes 131104 | tf_op jit(solution)/shard_map/ppermute | solution.py:112
  174.4 5.4 %collective-permute-done.17 = bf16[128,256]{1,0:T(8,128)(2,1)S(1)} collective-permute-done((bf16[128,256]{1,0:T(8,128)(2,1)S(1)}, bf16[128,256]{1,0:T(8,128)(2,1)S(1)}, u32[]{:S(2)}, u32[]{:S(2)}) %collective-permute-start.17) | collective-permute-done | bytes 65568 | tf_op jit(solution)/shard_map/ppermute | solution.py:112
  181.2 1.7 collective-permute-start.26
  182.9 2.5 %collective-permute-done.18 = bf16[128,256]{1,0:T(8,128)(2,1)S(1)} collective-permute-done((bf16[128,256]{1,0:T(8,128)(2,1)S(1)}, bf16[128,256]{1,0:T(8,128)(2,1)S(1)}, u32[]{:S(2)}, u32[]{:S(2)}) %collective-permute-start.18) | collective-permute-done | bytes 65568 | tf_op jit(solution)/shard_map/ppermute | solution.py:112
  188.0 2.5 %collective-permute-done.19 = bf16[256,256]{1,0:T(8,128)(2,1)S(1)} collective-permute-done((bf16[256,256]{1,0:T(8,128)(2,1)S(1)}, bf16[256,256]{1,0:T(8,128)(2,1)S(1)}, u32[]{:S(2)}, u32[]{:S(2)}) %collective-permute-start.19) | collective-permute-done | bytes 131104 | tf_op jit(solution)/shard_map/ppermute | solution.py:112
  193.6 5.4 %collective-permute-done.20 = bf16[512,256]{1,0:T(8,128)(2,1)S(1)} collective-permute-done((bf16[512,256]{1,0:T(8,128)(2,1)S(1)}, bf16[512,256]{1,0:T(8,128)(2,1)S(1)}, u32[]{:S(2)}, u32[]{:S(2)}) %collective-permute-start.20) | collective-permute-done | bytes 262176 | tf_op jit(solution)/shard_map/ppermute | solution.py:112
  202.4 6.1 %collective-permute-done.21 = bf16[1024,256]{1,0:T(8,128)(2,1)S(1)} collective-permute-done((bf16[1024,256]{1,0:T(8,128)(2,1)S(1)}, bf16[1024,256]{1,0:T(8,128)(2,1)S(1)}, u32[]{:S(2)}, u32[]{:S(2)}) %collective-permute-start.21) | collective-permute-done | bytes 524320 | tf_op jit(solution)/shard_map/ppermute | solution.py:112
  210.7 4.2 %collective-permute-done.30.got_ref = bf16[4096,256]{1,0:T(8,128)(2,1)} collective-permute-done((bf16[4096,256]{1,0:T(8,128)(2,1)S(1)}, bf16[4096,256]{1,0:T(8,128)(2,1)}, u32[]{:S(2)}, u32[]{:S(2)}) %collective-permute-start.30) | collective-permute-done | bytes 2097184 | tf_op jit(solution)/shard_map/ppermute | solution.py:112
  215.0 21.1 %shard_map.52 = bf16[1024,8192]{1,0:T(8,128)(2,1)} custom-call(s32[1]{0:T(128)} %bitcast.5.mine_ref, bf16[1024,256]{1,0:T(8,128)(2,1)S(1)} %convolution_convert_fusion.basis_ref, bf16[4096,256]{1,0:T(8,128)(2,1)S(1)} %pad_maximum_fusion.held_ref, bf16[4096,256]{1,0:T(8,128)(2,1)} %collective-permute-done.30.got_ref, bf16[1024,8192]{1,0:T(8,128)(2,1)} %fusion.adjusted_ref), custom_call_target="tpu_custom_call" | custom-call | flops 4294967296 | bytes 33554432 | tf_op jit(solution)/shard_map/pallas_call | solution.py:99
  236.1 2.1 select_convert_fusion
  (97 shorter events, 41.6 us)
Async XLA Ops:
  1.7 9.3 %collective-permute-start = (bf16[1,1,1,512,256]{4,3,2,1,0:T(8,128)(2,1)S(1)}, bf16[1,1,1,512,256]{4,3,2,1,0:T(8,128)(2,1)S(1)}, u32[]{:S(2)}, u32[]{:S(2)}) collective-permute-start(bf16[1,1,1,512,256]{4,3,2,1,0:T(8,128)(2,1)S(1)} %get-tuple-element.35), channel_id=1, source_target_pairs={{0,2},{1,3},{2,0},{3,1},{4,6},{5,7},{6,4},{7,5},{8,10},{9,11},{10,... | collective-permute-start | bytes 786440 | tf_op jit(solution)/shard_map/ppermute | solution.py:112
  4.7 7.8 %collective-permute-start.2 = (bf16[1,1,1,512,256]{4,3,2,1,0:T(8,128)(2,1)S(1)}, bf16[1,1,1,512,256]{4,3,2,1,0:T(8,128)(2,1)S(1)}, u32[]{:S(2)}, u32[]{:S(2)}) collective-permute-start(bf16[1,1,1,512,256]{4,3,2,1,0:T(8,128)(2,1)S(1)} %get-tuple-element.34), channel_id=1, source_target_pairs={{0,4},{1,5},{2,6},{3,7},{4,0},{5,1},{6,2},{7,3},{8,12},{9,13},{10,... | collective-permute-start | bytes 786440 | tf_op jit(solution)/shard_map/ppermute | solution.py:112
  13.6 20.5 %collective-permute-start.3 = (bf16[2,1,1,512,256]{4,3,2,1,0:T(8,128)(2,1)S(1)}, bf16[2,1,1,512,256]{4,3,2,1,0:T(8,128)(2,1)S(1)}, u32[]{:S(2)}, u32[]{:S(2)}) collective-permute-start(bf16[2,1,1,512,256]{4,3,2,1,0:T(8,128)(2,1)S(1)} %pad_maximum_fusion.4), channel_id=1, source_target_pairs={{0,2},{1,3},{2,0},{3,1},{4,6},{5,7},{6,4},{7,5},{8,10},{9,11},{10,... | collective-permute-start | bytes 1572872 | tf_op jit(solution)/shard_map/ppermute | solution.py:112
  14.1 20.1 %collective-permute-start.1 = (bf16[1,2,1,512,256]{4,3,2,1,0:T(8,128)(2,1)S(1)}, bf16[1,2,1,512,256]{4,3,2,1,0:T(8,128)(2,1)S(1)}, u32[]{:S(2)}, u32[]{:S(2)}) collective-permute-start(bf16[1,2,1,512,256]{4,3,2,1,0:T(8,128)(2,1)S(1)} %pad_maximum_fusion.3), channel_id=1, source_target_pairs={{0,4},{1,5},{2,6},{3,7},{4,0},{5,1},{6,2},{7,3},{8,12},{9,13},{10,... | collective-permute-start | bytes 1572872 | tf_op jit(solution)/shard_map/ppermute | solution.py:112
  34.5 3.6 %collective-permute-start.4 = (bf16[2,2,1,512,256]{4,3,2,1,0:T(8,128)(2,1)S(1)}, bf16[2,2,1,512,256]{4,3,2,1,0:T(8,128)(2,1)}, u32[]{:S(2)}, u32[]{:S(2)}) collective-permute-start(bf16[2,2,1,512,256]{4,3,2,1,0:T(8,128)(2,1)S(1)} %get-tuple-element.6), channel_id=1, source_target_pairs={{0,1},{1,0},{2,3},{3,2},{4,5},{5,4},{6,7},{7,6},{8,9},{9,8},{10,11... | collective-permute-start | bytes 3145736 | tf_op jit(solution)/shard_map/ppermute | solution.py:112
  34.5 5.0 %collective-permute-start.5 = (bf16[2,2,1,512,256]{4,3,2,1,0:T(8,128)(2,1)S(1)}, bf16[2,2,1,512,256]{4,3,2,1,0:T(8,128)(2,1)S(1)}, u32[]{:S(2)}, u32[]{:S(2)}) collective-permute-start(bf16[2,2,1,512,256]{4,3,2,1,0:T(8,128)(2,1)S(1)} %get-tuple-element.7), channel_id=1, source_target_pairs={{0,1},{1,0},{2,3},{3,2},{4,5},{5,4},{6,7},{7,6},{8,9},{9,8},{10,11... | collective-permute-start | bytes 3145736 | tf_op jit(solution)/shard_map/ppermute | solution.py:112
  38.0 6.1 %copy-start = (bf16[1024,8192]{1,0:T(8,128)(2,1)S(1)}, bf16[1024,8192]{1,0:T(8,128)(2,1)}, u32[]{:S(2)}) copy-start(bf16[1024,8192]{1,0:T(8,128)(2,1)} %fusion.adjusted_ref) | copy-start | bytes 50331652
  48.6 8.4 %collective-permute-start.6 = (bf16[512,256]{1,0:T(8,128)(2,1)S(1)}, bf16[512,256]{1,0:T(8,128)(2,1)S(1)}, u32[]{:S(2)}, u32[]{:S(2)}) collective-permute-start(bf16[512,256]{1,0:T(8,128)(2,1)S(1)} %dynamic-slice_convert_fusion.5), channel_id=1, source_target_pairs={{0,8},{8,0},{16,24},{24,16},{1,9},{9,1},{17,25},{25,17},{2,10},{10... | collective-permute-start | bytes 786440 | tf_op jit(solution)/shard_map/ppermute | solution.py:112
  57.1 8.5 %collective-permute-start.7 = (bf16[256,256]{1,0:T(8,128)(2,1)S(1)}, bf16[256,256]{1,0:T(8,128)(2,1)S(1)}, u32[]{:S(2)}, u32[]{:S(2)}) collective-permute-start(bf16[256,256]{1,0:T(8,128)(2,1)S(1)} %dynamic-slice_convert_fusion.8), channel_id=1, source_target_pairs={{0,16},{8,24},{16,0},{24,8},{1,17},{9,25},{17,1},{25,9},{2,18},{10... | collective-permute-start | bytes 393224 | tf_op jit(solution)/shard_map/ppermute | solution.py:112
  65.7 8.5 %collective-permute-start.8 = (bf16[256,256]{1,0:T(8,128)(2,1)S(1)}, bf16[256,256]{1,0:T(8,128)(2,1)S(1)}, u32[]{:S(2)}, u32[]{:S(2)}) collective-permute-start(bf16[256,256]{1,0:T(8,128)(2,1)S(1)} %add_convert_fusion.1), channel_id=1, source_target_pairs={{0,16},{8,24},{16,0},{24,8},{1,17},{9,25},{17,1},{25,9},{2,18},{10... | collective-permute-start | bytes 393224 | tf_op jit(solution)/shard_map/ppermute | solution.py:112
  74.3 6.4 %collective-permute-start.9 = (bf16[512,256]{1,0:T(8,128)(2,1)S(1)}, bf16[512,256]{1,0:T(8,128)(2,1)S(1)}, u32[]{:S(2)}, u32[]{:S(2)}) collective-permute-start(bf16[512,256]{1,0:T(8,128)(2,1)S(1)} %pad_maximum_fusion.10), channel_id=1, source_target_pairs={{0,8},{8,0},{16,24},{24,16},{1,9},{9,1},{17,25},{25,17},{2,10},{10... | collective-permute-start | bytes 786440 | tf_op jit(solution)/shard_map/ppermute | solution.py:112
  81.1 1.6 collective-permute-start.10
  82.8 8.4 %collective-permute-start.11 = (f32[256,256]{1,0:T(8,128)S(1)}, f32[256,256]{1,0:T(8,128)S(1)}, u32[]{:S(2)}, u32[]{:S(2)}) collective-permute-start(f32[256,256]{1,0:T(8,128)S(1)} %add.169), channel_id=1, source_target_pairs={{0,2},{1,3},{2,0},{3,1},{4,6},{5,7},{6,4},{7,5},{8,10},{9,11},{10,... | collective-permute-start | bytes 786440 | tf_op jit(solution)/shard_map/ppermute | solution.py:112
  91.2 7.6 %collective-permute-start.12 = (f32[256,256]{1,0:T(8,128)S(1)}, f32[256,256]{1,0:T(8,128)S(1)}, u32[]{:S(2)}, u32[]{:S(2)}) collective-permute-start(f32[256,256]{1,0:T(8,128)S(1)} %add.170), channel_id=1, source_target_pairs={{0,4},{1,5},{2,6},{3,7},{4,0},{5,1},{6,2},{7,3},{8,12},{9,13},{10,... | collective-permute-start | bytes 786440 | tf_op jit(solution)/shard_map/ppermute | solution.py:112
  133.3 4.4 %collective-permute-start.13 = (bf16[4096,256]{1,0:T(8,128)(2,1)S(1)}, bf16[4096,256]{1,0:T(8,128)(2,1)}, u32[]{:S(2)}, u32[]{:S(2)}) collective-permute-start(bf16[4096,256]{1,0:T(8,128)(2,1)S(1)} %dynamic-slice_convert_fusion), channel_id=1, source_target_pairs={{0,1},{1,0},{2,3},{3,2},{4,5},{5,4},{6,7},{7,6},{8,9},{9,8},{10,11... | collective-permute-start | bytes 6291464 | tf_op jit(solution)/shard_map/ppermute | solution.py:112
  142.5 14.1 %collective-permute-start.14 = (bf16[1024,256]{1,0:T(8,128)(2,1)S(1)}, bf16[1024,256]{1,0:T(8,128)(2,1)}, u32[]{:S(2)}, u32[]{:S(2)}) collective-permute-start(bf16[1024,256]{1,0:T(8,128)(2,1)S(1)} %dynamic-slice_convert_fusion.2), channel_id=1, source_target_pairs={{0,2},{1,3},{2,0},{3,1},{4,6},{5,7},{6,4},{7,5},{8,10},{9,11},{10,... | collective-permute-start | bytes 1572872 | tf_op jit(solution)/shard_map/ppermute | solution.py:112
  144.9 14.0 %collective-permute-start.22 = (bf16[1024,256]{1,0:T(8,128)(2,1)}, bf16[1024,256]{1,0:T(8,128)(2,1)}, u32[]{:S(2)}, u32[]{:S(2)}) collective-permute-start(bf16[1024,256]{1,0:T(8,128)(2,1)} %dynamic-slice_convert_fusion.1), channel_id=1, source_target_pairs={{0,4},{1,5},{2,6},{3,7},{4,0},{5,1},{6,2},{7,3},{8,12},{9,13},{10,... | collective-permute-start | bytes 1572872 | tf_op jit(solution)/shard_map/ppermute | solution.py:112
  158.2 7.6 %collective-permute-start.15 = (bf16[512,256]{1,0:T(8,128)(2,1)S(1)}, bf16[512,256]{1,0:T(8,128)(2,1)S(1)}, u32[]{:S(2)}, u32[]{:S(2)}) collective-permute-start(bf16[512,256]{1,0:T(8,128)(2,1)S(1)} %dynamic-slice_convert_fusion.4), channel_id=1, source_target_pairs={{0,4},{1,5},{2,6},{3,7},{4,0},{5,1},{6,2},{7,3},{8,12},{9,13},{10,... | collective-permute-start | bytes 786440 | tf_op jit(solution)/shard_map/ppermute | solution.py:112
  160.1 7.3 %collective-permute-start.23 = (bf16[512,256]{1,0:T(8,128)(2,1)S(1)}, bf16[512,256]{1,0:T(8,128)(2,1)S(1)}, u32[]{:S(2)}, u32[]{:S(2)}) collective-permute-start(bf16[512,256]{1,0:T(8,128)(2,1)S(1)} %dynamic-slice_convert_fusion.3), channel_id=1, source_target_pairs={{0,2},{1,3},{2,0},{3,1},{4,6},{5,7},{6,4},{7,5},{8,10},{9,11},{10,... | collective-permute-start | bytes 786440 | tf_op jit(solution)/shard_map/ppermute | solution.py:112
  165.9 5.3 %collective-permute-start.16 = (bf16[256,256]{1,0:T(8,128)(2,1)S(1)}, bf16[256,256]{1,0:T(8,128)(2,1)S(1)}, u32[]{:S(2)}, u32[]{:S(2)}) collective-permute-start(bf16[256,256]{1,0:T(8,128)(2,1)S(1)} %dynamic-slice_convert_fusion.7), channel_id=1, source_target_pairs={{0,8},{8,0},{16,24},{24,16},{1,9},{9,1},{17,25},{25,17},{2,10},{10... | collective-permute-start | bytes 393224 | tf_op jit(solution)/shard_map/ppermute | solution.py:112
  167.5 5.8 %collective-permute-start.24 = (bf16[256,256]{1,0:T(8,128)(2,1)S(1)}, bf16[256,256]{1,0:T(8,128)(2,1)S(1)}, u32[]{:S(2)}, u32[]{:S(2)}) collective-permute-start(bf16[256,256]{1,0:T(8,128)(2,1)S(1)} %dynamic-slice_convert_fusion.6), channel_id=1, source_target_pairs={{0,8},{8,0},{16,24},{24,16},{1,9},{9,1},{17,25},{25,17},{2,10},{10... | collective-permute-start | bytes 393224 | tf_op jit(solution)/shard_map/ppermute | solution.py:112
  171.2 8.6 %collective-permute-start.17 = (bf16[128,256]{1,0:T(8,128)(2,1)S(1)}, bf16[128,256]{1,0:T(8,128)(2,1)S(1)}, u32[]{:S(2)}, u32[]{:S(2)}) collective-permute-start(bf16[128,256]{1,0:T(8,128)(2,1)S(1)} %dynamic-slice_convert_fusion.10), channel_id=1, source_target_pairs={{0,16},{8,24},{16,0},{24,8},{1,17},{9,25},{17,1},{25,9},{2,18},{10... | collective-permute-start | bytes 196616 | tf_op jit(solution)/shard_map/ppermute | solution.py:112
  173.3 7.9 %collective-permute-start.25 = (bf16[128,256]{1,0:T(8,128)(2,1)S(1)}, bf16[128,256]{1,0:T(8,128)(2,1)S(1)}, u32[]{:S(2)}, u32[]{:S(2)}) collective-permute-start(bf16[128,256]{1,0:T(8,128)(2,1)S(1)} %dynamic-slice_convert_fusion.9), channel_id=1, source_target_pairs={{0,16},{8,24},{16,0},{24,8},{1,17},{9,25},{17,1},{25,9},{2,18},{10... | collective-permute-start | bytes 196616 | tf_op jit(solution)/shard_map/ppermute | solution.py:112
  179.8 5.6 %collective-permute-start.18 = (bf16[128,256]{1,0:T(8,128)(2,1)S(1)}, bf16[128,256]{1,0:T(8,128)(2,1)S(1)}, u32[]{:S(2)}, u32[]{:S(2)}) collective-permute-start(bf16[128,256]{1,0:T(8,128)(2,1)S(1)} %multiply_convert_fusion.1), channel_id=1, source_target_pairs={{0,16},{8,24},{16,0},{24,8},{1,17},{9,25},{17,1},{25,9},{2,18},{10... | collective-permute-start | bytes 196616 | tf_op jit(solution)/shard_map/ppermute | solution.py:112
  181.2 5.3 %collective-permute-start.26 = (bf16[128,256]{1,0:T(8,128)(2,1)S(1)}, bf16[128,256]{1,0:T(8,128)(2,1)S(1)}, u32[]{:S(2)}, u32[]{:S(2)}) collective-permute-start(bf16[128,256]{1,0:T(8,128)(2,1)S(1)} %multiply_convert_fusion), channel_id=1, source_target_pairs={{0,16},{8,24},{16,0},{24,8},{1,17},{9,25},{17,1},{25,9},{2,18},{10... | collective-permute-start | bytes 196616 | tf_op jit(solution)/shard_map/ppermute | solution.py:112
  185.5 5.0 %collective-permute-start.19 = (bf16[256,256]{1,0:T(8,128)(2,1)S(1)}, bf16[256,256]{1,0:T(8,128)(2,1)S(1)}, u32[]{:S(2)}, u32[]{:S(2)}) collective-permute-start(bf16[256,256]{1,0:T(8,128)(2,1)S(1)} %pad_maximum_fusion.13), channel_id=1, source_target_pairs={{0,8},{8,0},{16,24},{24,16},{1,9},{9,1},{17,25},{25,17},{2,10},{10... | collective-permute-start | bytes 393224 | tf_op jit(solution)/shard_map/ppermute | solution.py:112
  186.6 5.4 %collective-permute-start.27 = (bf16[256,256]{1,0:T(8,128)(2,1)S(1)}, bf16[256,256]{1,0:T(8,128)(2,1)S(1)}, u32[]{:S(2)}, u32[]{:S(2)}) collective-permute-start(bf16[256,256]{1,0:T(8,128)(2,1)S(1)} %pad_maximum_fusion.14), channel_id=1, source_target_pairs={{0,8},{8,0},{16,24},{24,16},{1,9},{9,1},{17,25},{25,17},{2,10},{10... | collective-permute-start | bytes 393224 | tf_op jit(solution)/shard_map/ppermute | solution.py:112
  190.6 8.5 %collective-permute-start.20 = (bf16[512,256]{1,0:T(8,128)(2,1)S(1)}, bf16[512,256]{1,0:T(8,128)(2,1)S(1)}, u32[]{:S(2)}, u32[]{:S(2)}) collective-permute-start(bf16[512,256]{1,0:T(8,128)(2,1)S(1)} %pad_maximum_fusion.11), channel_id=1, source_target_pairs={{0,4},{1,5},{2,6},{3,7},{4,0},{5,1},{6,2},{7,3},{8,12},{9,13},{10,... | collective-permute-start | bytes 786440 | tf_op jit(solution)/shard_map/ppermute | solution.py:112
  192.1 8.8 %collective-permute-start.28 = (bf16[512,256]{1,0:T(8,128)(2,1)S(1)}, bf16[512,256]{1,0:T(8,128)(2,1)S(1)}, u32[]{:S(2)}, u32[]{:S(2)}) collective-permute-start(bf16[512,256]{1,0:T(8,128)(2,1)S(1)} %pad_maximum_fusion.12), channel_id=1, source_target_pairs={{0,2},{1,3},{2,0},{3,1},{4,6},{5,7},{6,4},{7,5},{8,10},{9,11},{10,... | collective-permute-start | bytes 786440 | tf_op jit(solution)/shard_map/ppermute | solution.py:112
  199.2 9.2 %collective-permute-start.21 = (bf16[1024,256]{1,0:T(8,128)(2,1)S(1)}, bf16[1024,256]{1,0:T(8,128)(2,1)S(1)}, u32[]{:S(2)}, u32[]{:S(2)}) collective-permute-start(bf16[1024,256]{1,0:T(8,128)(2,1)S(1)} %pad_maximum_fusion.6), channel_id=1, source_target_pairs={{0,2},{1,3},{2,0},{3,1},{4,6},{5,7},{6,4},{7,5},{8,10},{9,11},{10,... | collective-permute-start | bytes 1572872 | tf_op jit(solution)/shard_map/ppermute | solution.py:112
  201.0 9.2 %collective-permute-start.29 = (bf16[1024,256]{1,0:T(8,128)(2,1)S(1)}, bf16[1024,256]{1,0:T(8,128)(2,1)S(1)}, u32[]{:S(2)}, u32[]{:S(2)}) collective-permute-start(bf16[1024,256]{1,0:T(8,128)(2,1)S(1)} %pad_maximum_fusion.7), channel_id=1, source_target_pairs={{0,4},{1,5},{2,6},{3,7},{4,0},{5,1},{6,2},{7,3},{8,12},{9,13},{10,... | collective-permute-start | bytes 1572872 | tf_op jit(solution)/shard_map/ppermute | solution.py:112
  210.6 4.4 %collective-permute-start.30 = (bf16[4096,256]{1,0:T(8,128)(2,1)S(1)}, bf16[4096,256]{1,0:T(8,128)(2,1)}, u32[]{:S(2)}, u32[]{:S(2)}) collective-permute-start(bf16[4096,256]{1,0:T(8,128)(2,1)S(1)} %pad_maximum_fusion.held_ref), channel_id=1, source_target_pairs={{0,1},{1,0},{2,3},{3,2},{4,5},{5,4},{6,7},{7,6},{8,9},{9,8},{10,11... | collective-permute-start | bytes 6291464 | tf_op jit(solution)/shard_map/ppermute | solution.py:112
  (1 other events, 1.3 us)
